TPU v7x, 768 devices: a whole 4x8x12 slice. The times are simulated.
768 devices in a mesh: gx: 4 (over x), gy: 24 (over z, core), gz: 8 (over y).
Axes of the slice: x: 4, y: 8, z: 12, core: 2. Of those that a mesh axis runs over, the one named last changes fastest.
Arguments:
- fine_state: float32 [14, 32, 192, 1024], P(None, 'gx', 'gy', 'gz'), may hold values from -5 to 5, as said below
- diffusivity: float32 [14], replicated, may hold values from 0.2 to 1.5
- coarse_cells: float32 [14, 98304], P(None, ('gx', 'gy', 'gz')), may hold values from -5 to 5, as said below
- copy_sources: int32 [4, 24, 8, 96, 3], P('gx', 'gy', 'gz'), may hold values from -1 to 127, as said below
- copy_targets: int32 [4, 24, 8, 96, 3], P('gx', 'gy', 'gz'), may hold values from -1 to 255, as said below
Outputs:
- section_state: float32 [14, 32, 192, 1024], P(None, 'gx', 'gy', 'gz')
Inputs may be any that keep to these rules, and one draw needn't show every extreme that they name: `fine_state`: field 9 (density) lies between 0.5 and 2. `coarse_cells`: field 9 (density) lies between 0.5 and 2. `copy_sources`: entry [a, b, c, p, s] is the row, among the 128 coarse cells of device (a, b, c), sent to peer p in slot s, or -1 for an empty slot; devices at the two x ends receive exactly 256 coarse cells each over all slots, the others none. `copy_targets`: entry [a, b, c, p, s] is the face cell of device (a, b, c) that slot s from peer p fills, or -1; it is -1 exactly where the matching copy_sources entry is; at the two x ends every face cell is filled once.
All inputs are finite; a program needn't handle non-finite values.
Results may differ from a plain program's by a relative error of at most 0.00002.
Values sent between devices are 32-bit elements; how exact they have to be, the bound alone decides.
A program may use at most 32 MiB of HBM per device.

v0:
```python
import jax
import jax.numpy as jnp
from jax import lax
from jax.sharding import PartitionSpec as P

time_step = 0.15


def extended(value, sides, width, wrap):
    for axis, dim in sides:
        count, length = (lax.axis_size(axis), value.shape[dim])
        up = [(i, (i + 1) % count) for i in range(count if wrap else count - 1)]
        down = [(j, i) for i, j in up]
        last = lax.slice_in_dim(value, length - width, length, axis=dim)
        leading = lax.slice_in_dim(value, 0, width, axis=dim)
        before = lax.ppermute(last, axis, up)
        after = lax.ppermute(leading, axis, down)
        value = jnp.concatenate([before, value, after], axis=dim)
    return value


def face_divergence(padded, direction, diffusivity):
    face_count = padded.shape[direction] - 3

    def planes_at(offset):
        return lax.slice_in_dim(padded, offset, offset + face_count, axis=direction)

    left_far, left_cell, right_cell, right_far = (
        planes_at(0),
        planes_at(1),
        planes_at(2),
        planes_at(3),
    )
    component = 9 + direction
    rho_left = left_cell[9:10]
    rho_right = right_cell[9:10]
    velocity = 0.5 * (
        left_cell[component : component + 1] / rho_left
        + right_cell[component : component + 1] / rho_right
    )
    from_left = left_cell + 0.25 * (right_cell - left_far)
    from_right = right_cell - 0.25 * (right_far - left_cell)
    advect = jnp.maximum(velocity, 0.0) * from_left + jnp.minimum(velocity, 0.0) * from_right
    spread = (
        diffusivity.reshape(-1, 1, 1, 1)
        * (0.5 * (rho_left + rho_right))
        * (right_cell / rho_right - left_cell / rho_left)
    )
    face_flux = advect - spread
    cell_count = face_count - 1
    return lax.slice_in_dim(face_flux, 1, cell_count + 1, axis=direction) - lax.slice_in_dim(
        face_flux, 0, cell_count, axis=direction
    )


def on_device(fine_state, diffusivity, coarse_cells, copy_sources, copy_targets):
    fields, cells_x, cells_y, cells_z = fine_state.shape
    wanted = copy_sources[0, 0, 0]
    picked = jnp.take(coarse_cells, jnp.maximum(wanted, 0), axis=1)
    picked = jnp.where(wanted[None] >= 0, picked, 0.0)
    arrived = lax.all_to_all(picked, ("gx", "gy"), split_axis=1, concat_axis=1, tiled=True)
    half_cells = cells_y // 2 * (cells_z // 2)
    target = copy_targets[0, 0, 0]
    target = jnp.where(target >= 0, target, half_cells).reshape(-1)
    coarse_plane = (
        jnp.zeros((fields, half_cells + 1), jnp.float32)
        .at[:, target]
        .add(arrived.reshape(fields, -1))
    )
    coarse_plane = coarse_plane[:, :half_cells].reshape(fields, cells_y // 2, 1, cells_z // 2, 1)
    fine_plane = jnp.broadcast_to(coarse_plane, (fields, cells_y // 2, 2, cells_z // 2, 2)).reshape(
        fields, cells_y, cells_z
    )
    ghost_layer = jnp.broadcast_to(fine_plane[:, None], (fields, 2, cells_y, cells_z))
    index_x = lax.axis_index("gx")
    width_x = lax.axis_size("gx")
    along_x = extended(fine_state, (("gx", 1),), 2, False)
    along_yz = extended(fine_state, (("gy", 2), ("gz", 3)), 2, True)
    along_y = along_yz[:, :, :, 2:-2]
    along_z = along_yz[:, :, 2:-2, :]
    low_side = jnp.where(index_x == 0, ghost_layer, along_x[:, :2])
    high_side = jnp.where(index_x == width_x - 1, ghost_layer, along_x[:, -2:])
    along_x = jnp.concatenate([low_side, along_x[:, 2:-2], high_side], axis=1)
    divergence = face_divergence(along_x, 1, diffusivity)
    divergence = divergence + face_divergence(along_y, 2, diffusivity)
    divergence = divergence + face_divergence(along_z, 3, diffusivity)
    return fine_state - time_step * divergence


def solution(mesh):
    return jax.shard_map(
        on_device,
        mesh=mesh,
        in_specs=(
            P(None, "gx", "gy", "gz"),
            P(),
            P(None, ("gx", "gy", "gz")),
            P("gx", "gy", "gz", None, None),
            P("gx", "gy", "gz", None, None),
        ),
        out_specs=P(None, "gx", "gy", "gz"),
        check_vma=False,
    )
```

profile of v0, /device:TPU:26, one launch (start us, length us, event | category | flops | bytes accessed | tf_op | source)
XLA Modules:
  0.0 73.1 jit_solution(17089304684554108616)
XLA Ops:
  0.0 1.3 %fusion.48 = (f32[14,8,2,128]{3,2,1,0:T(2,128)S(1)}, f32[14,8,2,128]{3,2,1,0:T(2,128)S(1)}) fusion(f32[14,8,8,128]{3,2,1,0:T(8,128)} %param.5), kind=kLoop, calls=%fused_computation.96 | loop fusion | bytes 458752 | tf_op jit(solution)/shard_map/slice | solution.py:14
  1.3 12.1 %collective-permute-start.3 = (f32[14,8,2,128]{3,2,1,0:T(2,128)S(1)}, f32[14,8,2,128]{3,2,1,0:T(2,128)S(1)}, u32[]{:S(2)}, u32[]{:S(2)}) collective-permute-start(f32[14,8,2,128]{3,2,1,0:T(2,128)S(1)} %get-tuple-element.25), channel_id=1, source_target_pairs={{8,0},{16,8},{24,16},{32,24},{40,32},{48,40},{56,48},{64,56},{72,6... | collective-permute-start | bytes 344072 | tf_op jit(solution)/shard_map/ppermute | solution.py:17
  13.4 1.7 %fusion.47 = (f32[14,2,8,128]{3,2,1,0:T(8,128)}, f32[14,2,8,128]{3,2,1,0:T(8,128)}) fusion(f32[14,8,8,128]{3,2,1,0:T(8,128)} %param.5), kind=kLoop, calls=%fused_computation.95 | loop fusion | bytes 458752 | tf_op jit(solution)/shard_map/slice | solution.py:14
  15.1 3.4 %collective-permute-start = (f32[14,2,8,128]{3,2,1,0:T(8,128)}, f32[14,2,8,128]{3,2,1,0:T(8,128)}, u32[]{:S(2)}, u32[]{:S(2)}) collective-permute-start(f32[14,2,8,128]{3,2,1,0:T(8,128)} %get-tuple-element.22), channel_id=1, source_target_pairs={{0,192},{192,384},{384,576},{1,193},{193,385},{385,577},{2,194},{1... | collective-permute-start | bytes 344072 | tf_op jit(solution)/shard_map/ppermute | solution.py:16
  19.2 0.7 broadcast_compare_fusion
  19.9 0.8 %copy.36 = f32[14,128]{0,1:T(8,128)S(1)} copy(f32[14,128]{1,0:T(8,128)} %param.7) | data formatting | bytes 14336 | tf_op args[2]
  21.0 1.1 %gather_fusion = f32[288,14]{1,0:T(8,128)S(1)} fusion(f32[14,128]{0,1:T(8,128)S(1)} %copy.36, s32[1024]{0:T(1024)S(1)} %pad_clamp_fusion), kind=kCustom, calls=%fused_computation | custom fusion | bytes 33408 | tf_op jit(solution)/shard_map/jit(_take)/gather | solution.py:59
  22.4 0.9 %select_bitcast_fusion = f32[14,96,3]{0,2,1:T(4,128)} fusion(f32[96,3,14]{2,1,0:T(4,128)S(1)} %reshape.77, pred[96,3]{1,0:T(8,128)(4,1)S(1)} %bitcast.47, pred[96,3]{1,0:T(8,128)(4,1)S(1)} %bitcast.48), kind=kLoop, calls=%fused_computation.52 | loop fusion | flops 8064 | bytes 32832 | tf_op jit(solution)/shard_map/jit(_where)/select_n | solution.py:60
  23.3 8.8 %all-to-all-start = ((f32[14,96,3]{0,2,1:T(4,128)}), f32[14,96,3]{0,2,1:T(4,128)S(1)}, u32[]{:S(2)}, u32[]{:S(2)}) async-start(f32[14,96,3]{0,2,1:T(4,128)} %select_bitcast_fusion), calls=%async_computation | async-start | bytes 393216 | tf_op jit(solution)/shard_map/all_to_all | solution.py:61
  32.1 2.5 %collective-permute-start.1 = (f32[14,2,8,128]{3,2,1,0:T(8,128)}, f32[14,2,8,128]{3,2,1,0:T(8,128)}, u32[]{:S(2)}, u32[]{:S(2)}) collective-permute-start(f32[14,2,8,128]{3,2,1,0:T(8,128)} %get-tuple-element.23), channel_id=1, source_target_pairs={{192,0},{384,192},{576,384},{193,1},{385,193},{577,385},{194,2},{3... | collective-permute-start | bytes 344072 | tf_op jit(solution)/shard_map/ppermute | solution.py:17
  35.0 13.5 %all-to-all-done = f32[14,96,3]{0,2,1:T(4,128)S(1)} async-done(((f32[14,96,3]{0,2,1:T(4,128)}), f32[14,96,3]{0,2,1:T(4,128)S(1)}, u32[]{:S(2)}, u32[]{:S(2)}) %all-to-all-start) | async-done | bytes 16160 | tf_op jit(solution)/shard_map/all_to_all | solution.py:61
  48.6 2.6 %scatter_custom_fusion = f32[14,257]{0,1:T(8,128)S(1)} fusion(s32[288]{0:T(512)S(1)} %fusion.42, f32[14,288]{0,1:T(8,128)S(1)} %reshape.81, f32[]{:T(128)} %constant.15.clone.1), kind=kCustom, calls=%fused_computation.53 | custom fusion | flops 4032 | bytes 161852 | tf_op jit(solution)/shard_map/scatter-add | solution.py:68
  52.0 1.4 %copy.48 = f32[14,8,12,2]{0,1,3,2:T(8,128)} copy(f32[14,8,12,2]{3,2,1,0:T(8,128)S(1)} %get-tuple-element.18) | data formatting | bytes 21504 | tf_op jit(solution)/shard_map/slice | solution.py:14
  53.4 4.7 %collective-permute-start.4 = (f32[14,8,12,2]{0,1,3,2:T(8,128)}, f32[14,8,12,2]{0,1,3,2:T(8,128)}, u32[]{:S(2)}, u32[]{:S(2)}) collective-permute-start(f32[14,8,12,2]{0,1,3,2:T(8,128)} %copy.48), channel_id=1, source_target_pairs={{0,1},{1,2},{2,3},{3,4},{4,5},{5,6},{6,7},{7,0},{8,9},{9,10},{10,1... | collective-permute-start | bytes 32264 | tf_op jit(solution)/shard_map/ppermute | solution.py:16
  58.1 1.4 %copy.50 = f32[14,8,12,2]{0,1,3,2:T(8,128)} copy(f32[14,8,12,2]{3,2,1,0:T(8,128)S(1)} %get-tuple-element.19) | data formatting | bytes 21504 | tf_op jit(solution)/shard_map/slice | solution.py:15
  59.5 1.9 %collective-permute-start.5 = (f32[14,8,12,2]{0,1,3,2:T(8,128)}, f32[14,8,12,2]{0,1,3,2:T(8,128)}, u32[]{:S(2)}, u32[]{:S(2)}) collective-permute-start(f32[14,8,12,2]{0,1,3,2:T(8,128)} %copy.50), channel_id=1, source_target_pairs={{1,0},{2,1},{3,2},{4,3},{5,4},{6,5},{7,6},{0,7},{9,8},{10,9},{11,1... | collective-permute-start | bytes 32264 | tf_op jit(solution)/shard_map/ppermute | solution.py:17
  61.5 1.0 %broadcast_select_fusion.1 = (f32[14,2,8,128]{3,2,1,0:T(8,128)S(1)}, f32[14,2,8,128]{3,2,1,0:T(8,128)S(1)}) fusion(f32[14,2,8,128]{3,2,1,0:T(8,128)} %collective-permute-done, f32[14,8,128]{2,1,0:T(8,128)S(1)} %copy.37, pred[]{:T(512)S(6)} %eq.6, f32[14,2,8,128]{3,2,1,0:T(8,128)} %collective-permute-done.1, pred[]{:T(512)S(6)} %eq.7), kind=kLoop, calls=%fused_computation.75 | loop fusion | flops 57344 | bytes 516098 | tf_op jit(solution)/shard_map/jit(_where)/select_n | solution.py:81
  62.6 1.6 %fusion.12 = f32[14,8,9,128]{3,2,1,0:T(8,128)} fusion(f32[14,8,10,128]{3,2,1,0:T(8,128)S(1)} %constant_dynamic-update-slice_fusion, f32[14,8,8,128]{3,2,1,0:T(8,128)S(1)} %copy-done, f32[14,8,2,128]{3,2,1,0:T(2,128)S(1)} %collective-permute-done.2, f32[8,9,128]{2,1,0:T(8,128)S(1)} %bitcast.43, f32[8,9,128]{2,1,0:T(8,128)S(1)} %get-tuple-element.17, ...), kind=kLoop, calls=%fused_computation.19 | loop fusion | flops 2193408 | bytes 2306104 | tf_op jit(solution)/shard_map/sub | solution.py:49
  64.5 2.0 %copy.49 = f32[14,8,12,2]{3,2,1,0:T(8,128)S(1)} copy(f32[14,8,12,2]{0,1,3,2:T(8,128)} %collective-permute-done.4) | data formatting | bytes 21504 | tf_op jit(solution)/shard_map/ppermute | solution.py:16
  66.5 1.0 %collective-permute-done.5 = f32[14,8,12,2]{0,1,3,2:T(8,128)} collective-permute-done((f32[14,8,12,2]{0,1,3,2:T(8,128)}, f32[14,8,12,2]{0,1,3,2:T(8,128)}, u32[]{:S(2)}, u32[]{:S(2)}) %collective-permute-start.5) | collective-permute-done | bytes 10784 | tf_op jit(solution)/shard_map/ppermute | solution.py:17
  67.5 2.0 %copy.51 = f32[14,8,12,2]{3,2,1,0:T(8,128)S(1)} copy(f32[14,8,12,2]{0,1,3,2:T(8,128)} %collective-permute-done.5) | data formatting | bytes 21504 | tf_op jit(solution)/shard_map/ppermute | solution.py:17
  69.7 1.2 %maximum_maximum_fusion = (f32[14,8,12,130]{3,2,1,0:T(8,128)S(1)}, f32[14,8,12,130]{3,2,1,0:T(8,128)S(1)}) fusion(f32[14,8,2,128]{3,2,1,0:T(2,128)S(1)} %collective-permute-done.3, f32[14,8,8,128]{3,2,1,0:T(8,128)S(1)} %copy-done, f32[14,8,2,128]{3,2,1,0:T(2,128)S(1)} %collective-permute-done.2, f32[14,8,12,2]{3,2,1,0:T(8,128)S(1)} %copy.49, ...), kind=kLoop, calls=%fused_computation.2 | loop fusion | flops 1048320 | bytes 2107392 | tf_op jit(solution)/shard_map/concatenate | solution.py:18
  71.0 0.8 %fusion.4 = f32[14,8,8,129]{3,2,1,0:T(8,128)S(1)} fusion(f32[14,8,12,130]{3,2,1,0:T(8,128)S(1)} %get-tuple-element.21, f32[14,8,12,130]{3,2,1,0:T(8,128)S(1)} %get-tuple-element.20, f32[8,8,129]{2,1,0:T(8,128)S(1)} %bitcast.42, f32[8,8,129]{2,1,0:T(8,128)S(1)} %bitcast.41, f32[8,8,129]{2,1,0:T(8,128)S(1)} %get-tuple-element.30, f32[14]{0:T(128)S(1)} %copy-done.2, ...), kind=kLoop, calls=%fused_computation.9 | loop fusion | flops 1733760 | bytes 2476856 | tf_op jit(solution)/shard_map/sub | solution.py:49
  72.1 1.0 %fusion.31 = f32[14,8,8,128]{3,2,1,0:T(8,128)} fusion(f32[14,8,8,128]{3,2,1,0:T(8,128)S(1)} %copy-done, f32[14,8,8,129]{3,2,1,0:T(8,128)S(1)} %fusion.4, f32[14,8,9,128]{3,2,1,0:T(8,128)S(1)} %copy-done.1, f32[14,9,8,128]{3,2,1,0:T(8,128)S(1)} %fusion.24), kind=kLoop, calls=%fused_computation.48 | loop fusion | flops 802816 | bytes 3670016 | tf_op jit(solution)/shard_map/sub | solution.py:87
  (40 shorter events, 3.5 us)
Async XLA Ops:
  1.3 50.2 %collective-permute-start.3 = (f32[14,8,2,128]{3,2,1,0:T(2,128)S(1)}, f32[14,8,2,128]{3,2,1,0:T(2,128)S(1)}, u32[]{:S(2)}, u32[]{:S(2)}) collective-permute-start(f32[14,8,2,128]{3,2,1,0:T(2,128)S(1)} %get-tuple-element.25), channel_id=1, source_target_pairs={{8,0},{16,8},{24,16},{32,24},{40,32},{48,40},{56,48},{64,56},{72,6... | collective-permute-start | bytes 344072 | tf_op jit(solution)/shard_map/ppermute | solution.py:17
  13.4 38.1 %collective-permute-start.2 = (f32[14,8,2,128]{3,2,1,0:T(2,128)S(1)}, f32[14,8,2,128]{3,2,1,0:T(2,128)S(1)}, u32[]{:S(2)}, u32[]{:S(2)}) collective-permute-start(f32[14,8,2,128]{3,2,1,0:T(2,128)S(1)} %get-tuple-element.24), channel_id=1, source_target_pairs={{0,8},{8,16},{16,24},{24,32},{32,40},{40,48},{48,56},{56,64},{64,7... | collective-permute-start | bytes 344072 | tf_op jit(solution)/shard_map/ppermute | solution.py:16
  15.1 46.4 %collective-permute-start = (f32[14,2,8,128]{3,2,1,0:T(8,128)}, f32[14,2,8,128]{3,2,1,0:T(8,128)}, u32[]{:S(2)}, u32[]{:S(2)}) collective-permute-start(f32[14,2,8,128]{3,2,1,0:T(8,128)} %get-tuple-element.22), channel_id=1, source_target_pairs={{0,192},{192,384},{384,576},{1,193},{193,385},{385,577},{2,194},{1... | collective-permute-start | bytes 344072 | tf_op jit(solution)/shard_map/ppermute | solution.py:16
  20.9 13.7 %copy-start = (f32[14,8,8,128]{3,2,1,0:T(8,128)S(1)}, f32[14,8,8,128]{3,2,1,0:T(8,128)}, u32[]{:S(2)}) copy-start(f32[14,8,8,128]{3,2,1,0:T(8,128)} %param.5) | copy-start | bytes 1376260
  22.0 12.7 %copy-start.3 = (s32[1,1,1,96,3]{3,2,4,1,0:T(1,128)S(1)}, s32[1,1,1,96,3]{3,2,4,1,0:T(1,128)}, u32[]{:S(2)}) copy-start(s32[1,1,1,96,3]{3,2,4,1,0:T(1,128)} %param.9) | copy-start | bytes 3460
  23.3 25.2 %all-to-all-start = ((f32[14,96,3]{0,2,1:T(4,128)}), f32[14,96,3]{0,2,1:T(4,128)S(1)}, u32[]{:S(2)}, u32[]{:S(2)}) async-start(f32[14,96,3]{0,2,1:T(4,128)} %select_bitcast_fusion), calls=%async_computation | async-start | bytes 393216 | tf_op jit(solution)/shard_map/all_to_all | solution.py:61
  32.1 29.4 %collective-permute-start.1 = (f32[14,2,8,128]{3,2,1,0:T(8,128)}, f32[14,2,8,128]{3,2,1,0:T(8,128)}, u32[]{:S(2)}, u32[]{:S(2)}) collective-permute-start(f32[14,2,8,128]{3,2,1,0:T(8,128)} %get-tuple-element.23), channel_id=1, source_target_pairs={{192,0},{384,192},{576,384},{193,1},{385,193},{577,385},{194,2},{3... | collective-permute-start | bytes 344072 | tf_op jit(solution)/shard_map/ppermute | solution.py:17
  53.4 11.1 %collective-permute-start.4 = (f32[14,8,12,2]{0,1,3,2:T(8,128)}, f32[14,8,12,2]{0,1,3,2:T(8,128)}, u32[]{:S(2)}, u32[]{:S(2)}) collective-permute-start(f32[14,8,12,2]{0,1,3,2:T(8,128)} %copy.48), channel_id=1, source_target_pairs={{0,1},{1,2},{2,3},{3,4},{4,5},{5,6},{6,7},{7,0},{8,9},{9,10},{10,1... | collective-permute-start | bytes 32264 | tf_op jit(solution)/shard_map/ppermute | solution.py:16
  58.1 4.5 %copy-start.2 = (f32[14]{0:T(128)S(1)}, f32[14]{0:T(128)}, u32[]{:S(2)}) copy-start(f32[14]{0:T(128)} %param.6) | copy-start | bytes 172
  59.5 8.0 %collective-permute-start.5 = (f32[14,8,12,2]{0,1,3,2:T(8,128)}, f32[14,8,12,2]{0,1,3,2:T(8,128)}, u32[]{:S(2)}, u32[]{:S(2)}) collective-permute-start(f32[14,8,12,2]{0,1,3,2:T(8,128)} %copy.50), channel_id=1, source_target_pairs={{1,0},{2,1},{3,2},{4,3},{5,4},{6,5},{7,6},{0,7},{9,8},{10,9},{11,1... | collective-permute-start | bytes 32264 | tf_op jit(solution)/shard_map/ppermute | solution.py:17
  71.0 1.2 %copy-start.1 = (f32[14,8,9,128]{3,2,1,0:T(8,128)S(1)}, f32[14,8,9,128]{3,2,1,0:T(8,128)}, u32[]{:S(2)}) copy-start(f32[14,8,9,128]{3,2,1,0:T(8,128)} %fusion.12) | copy-start | bytes 1548292
where the time goes:
time: 73.6 us; the launch traced here: 73.1 us
  starting transfers between devices  33.5 us (46%)
  waiting for transfers between devices  14.4 us (20%)
  local copies, waits for them, and re-layouts  13.6 us (18%)
  other arithmetic  11.3 us (15%)
    ppermute x3, starting transfers between devices, extended(): after = lax.ppermute(leading, axis, down)  16.6 us
    all_to_all x1, waiting for transfers between devices, on_device(): lax.all_to_all(picked, ('gx', 'gy'), split_axis=1, concat_axis=1, tiled=T...  13.5 us
    all_to_all x1, starting transfers between devices, on_device(): lax.all_to_all(picked, ('gx', 'gy'), split_axis=1, concat_axis=1, tiled=T...  8.8 us
    ppermute x3, starting transfers between devices, extended(): before = lax.ppermute(last, axis, up)  8.08 us
    slice x4, local copies, waits for them, and re-layouts, extended(): last = lax.slice_in_dim(value, length - width, length, axis=dim)  4.62 us
    sub x3, other arithmetic, face_divergence(): face_flux = advect - spread  2.71 us
    scatter-add x1, other arithmetic, on_device(): coarse_plane = jnp.zeros((fields, half_cells + 1), jnp.float32).at[:, tar...  2.58 us
    ppermute x1, local copies, waits for them, and re-layouts, extended(): before = lax.ppermute(last, axis, up)  2.03 us
  transfers between devices with their start and end apart: 7, of which 2 were waited for; matrix products, arithmetic and copies ran while one was open for 25% of the time, Pallas kernels for 0%

commit v1 on v0

v1 whole, which is shorter than its diff:
```python
import functools

import jax
import jax.numpy as jnp
from jax import lax
from jax.experimental import pallas as pl
from jax.experimental.pallas import tpu as pltpu
from jax.sharding import PartitionSpec as P

MESH = pl.DeviceIdType.MESH
time_step = 0.15
SLOT = 16


def split3(value):
    hi = value.astype(jnp.bfloat16)
    rest = value - hi.astype(jnp.float32)
    mid = rest.astype(jnp.bfloat16)
    low = (rest - mid.astype(jnp.float32)).astype(jnp.bfloat16)
    return jnp.concatenate([hi, mid, low], axis=0)


def face_terms(rho_left, rho_right, mom_left, mom_right):
    inv_left, inv_right = 1.0 / rho_left, 1.0 / rho_right
    velocity = (0.5 * time_step) * (mom_left * inv_left + mom_right * inv_right)
    up, down = jnp.maximum(velocity, 0.0), jnp.minimum(velocity, 0.0)
    quarter_up, quarter_down = 0.25 * up, 0.25 * down
    mean_rho = (0.5 * time_step) * (rho_left + rho_right)
    return (
        up + quarter_down,
        down + quarter_up,
        quarter_up,
        quarter_down,
        mean_rho * inv_left,
        mean_rho * inv_right,
    )


def face_flux(terms, diff, far_left, left, right, far_right):
    a_left, a_right, b_left, b_right, e_left, e_right = terms
    return (
        left * (a_left + diff * e_left)
        + right * (a_right - diff * e_right)
        - b_left * far_left
        - b_right * far_right
    )


def kernel(
    n_x, n_y, n_z, fields,
    fine, diff, coarse, sources, targets,
    out,
    qx, y_own, y_low, y_high, y_rows, y_flux, z_own, z_low, z_high, z_flux,
    cells, src, tgt, msg, first, second, arrived, order, spread, plane, terms,
    load_sem, halo_send, halo_recv, first_send, first_recv, second_send, second_recv,
):
    a, b, c = lax.axis_index("gx"), lax.axis_index("gy"), lax.axis_index("gz")
    is_end = jnp.logical_or(a == 0, a == n_x - 1)
    peers = n_x * n_y

    def x_at(k):
        return (lax.rem(a + (k + n_x), n_x), b, c)

    def y_at(k):
        return (a, lax.rem(b + (k + n_y), n_y), c)

    def z_at(k):
        return (a, b, lax.rem(c + (k + n_z), n_z))

    load_cells = pltpu.make_async_copy(coarse, cells, load_sem.at[0])
    load_src = pltpu.make_async_copy(sources, src, load_sem.at[1])
    load_fine = pltpu.make_async_copy(fine, qx.at[:, pl.ds(16, 64)], load_sem.at[2])
    load_tgt = pltpu.make_async_copy(targets, tgt, load_sem.at[3])
    load_cells.start()
    load_src.start()
    load_fine.start()
    load_tgt.start()

    barrier = pltpu.get_barrier_semaphore()

    def greet(device):
        pl.semaphore_signal(barrier, inc=1, device_id=device, device_id_type=MESH)

    for k in range(1, n_x):
        greet(x_at(k))
    greet(y_at(1))
    greet(y_at(-1))
    greet(z_at(1))
    greet(z_at(-1))

    @pl.when(is_end)
    def _():
        for k in range(2, n_y - 1):
            greet(y_at(k))

    load_cells.wait()
    load_src.wait()
    owned = jnp.concatenate([cells[...], jnp.zeros((SLOT - fields, 128), jnp.float32)], axis=0)
    owned = split3(owned)
    row = lax.broadcasted_iota(jnp.int32, (128, 128), 0)
    blank = jnp.full((1, 128 - peers), -1, jnp.int32)
    picked = []
    for s in range(3):
        wanted = jnp.concatenate([src[s], blank], axis=1)
        chosen = jnp.where(row == wanted, 1.0, 0.0).astype(jnp.bfloat16)
        part = jnp.dot(owned, chosen, preferred_element_type=jnp.float32)
        picked.append(part[:SLOT] + part[SLOT : 2 * SLOT] + part[2 * SLOT :])
    picked.append(jnp.zeros((128 - 3 * SLOT, 128), jnp.float32))
    picked = jnp.concatenate(picked, axis=0).T
    msg[0] = picked[:n_y]
    msg[1] = picked[peers - n_y : peers]

    load_fine.wait()
    lane = lax.broadcasted_iota(jnp.int32, (8, 128), 1)
    line = lax.broadcasted_iota(jnp.int32, (8, 128), 0)
    for f in range(fields):
        y_own[0, f, 0] = qx[f, pl.ds(16, 8, stride=8), :]
        y_own[0, f, 1] = qx[f, pl.ds(17, 8, stride=8), :]
        y_own[1, f, 0] = qx[f, pl.ds(22, 8, stride=8), :]
        y_own[1, f, 1] = qx[f, pl.ds(23, 8, stride=8), :]
        packed = pltpu.roll(qx[f, pl.ds(16, 8), :], 2, 1)
        for x in range(1, 8):
            moved = pltpu.roll(qx[f, pl.ds(16 + 8 * x, 8), :], 4 * x + 2, 1)
            packed = jnp.where(lane >= 4 * x, moved, packed)
        z_own[f] = packed

    @pl.when(is_end)
    def _():
        pl.semaphore_wait(barrier, n_x - 1 + n_y - 1 + 2)

    @pl.when(jnp.logical_not(is_end))
    def _():
        pl.semaphore_wait(barrier, n_x - 1 + 2 + 2)

    def to_end(which):
        end = (0, n_x - 1)[which]
        return pltpu.make_async_remote_copy(
            src_ref=msg.at[which], dst_ref=first.at[a],
            send_sem=first_send.at[which], recv_sem=first_recv.at[a],
            device_id=(end, b, c), device_id_type=MESH,
        )

    for which in range(2):
        end = (0, n_x - 1)[which]

        @pl.when(a != end)
        def _():
            to_end(which).start()

        @pl.when(a == end)
        def _():
            first[end] = msg[which]

    def halo(i, source, target, device):
        return pltpu.make_async_remote_copy(
            src_ref=source, dst_ref=target, send_sem=halo_send.at[i], recv_sem=halo_recv.at[i],
            device_id=device, device_id_type=MESH,
        )

    halos = [
        halo(0, y_own.at[0], y_high, y_at(-1)),
        halo(1, y_own.at[1], y_low, y_at(1)),
        halo(2, z_own, z_high, z_at(-1)),
        halo(3, z_own, z_low, z_at(1)),
        halo(4, qx.at[:, pl.ds(16, 16)], qx.at[:, pl.ds(80, 16)], x_at(-1)),
        halo(5, qx.at[:, pl.ds(64, 16)], qx.at[:, pl.ds(0, 16)], x_at(1)),
    ]
    for copy in halos:
        copy.start()

    load_tgt.wait()

    def to_peer(k):
        return pltpu.make_async_remote_copy(
            src_ref=second.at[pl.ds(pl.multiple_of(8 * lax.rem(b + k, n_y), 8), 8)], dst_ref=arrived.at[b],
            send_sem=second_send, recv_sem=second_recv,
            device_id=y_at(k), device_id_type=MESH,
        )

    @pl.when(is_end)
    def _():
        wide = [jnp.concatenate([tgt[s], blank], axis=1) for s in range(3)]
        wide.append(jnp.full((125, 128), -1, jnp.int32))
        wide = jnp.concatenate(wide, axis=0).astype(jnp.float32).T
        order[...] = jnp.full(order.shape, -1.0, jnp.float32)
        for k in range(n_x):
            order[pl.ds(k, n_y, stride=8), :] = wide[k * n_y : (k + 1) * n_y]
        half = (lax.broadcasted_iota(jnp.int32, (256, 128), 1) // 2).astype(jnp.float32)
        filled = order[...]
        for s in range(3):
            cell = filled[:, s : s + 1]
            for h in range(4):
                spread[256 * s : 256 * (s + 1), 128 * h : 128 * (h + 1)] = jnp.where(
                    cell - 64.0 * h == half, 1.0, 0.0
                ).astype(jnp.bfloat16)
        second[...] = jnp.zeros(second.shape, jnp.float32)
        if n_y < 32:
            arrived[n_y:] = jnp.zeros((32 - n_y, 8, 128), jnp.float32)
        for k in range(1, n_x):
            pltpu.make_async_remote_copy(
                src_ref=msg.at[0], dst_ref=first.at[lax.rem(a + k, n_x)],
                send_sem=first_send.at[0], recv_sem=first_recv.at[lax.rem(a + k, n_x)],
                device_id=x_at(k), device_id_type=MESH,
            ).wait_recv()
        for k in range(n_x):
            second[pl.ds(k, n_y, stride=8), :] = first[k]
        for k in range(1, n_y):
            to_peer(k).start()
        arrived[b] = second[pl.ds(pl.multiple_of(8 * b, 8), 8), :]

    for i in range(4):
        halos[i].wait_recv()

    def tile(f, x):
        return qx[f, pl.ds(16 + 8 * x, 8), :]

    def z_next(f, x):
        kept = jnp.where(lane % 4 < 2, z_low[f], z_high[f])
        return pltpu.roll(kept, 126 - 4 * x, 1)

    def shifted(value, beyond, index, size, axis):
        far_left = pltpu.roll(jnp.where(index >= size - 2, beyond, value), 2, axis)
        left = pltpu.roll(jnp.where(index == size - 1, beyond, value), 1, axis)
        far_right = pltpu.roll(jnp.where(index == 0, beyond, value), size - 1, axis)
        return far_left, left, far_right

    last_y = face_terms(y_own[1, 9, 1], y_high[9, 0], y_own[1, 11, 1], y_high[11, 0])

    def z_last(f):
        cells4 = jnp.where(lane % 4 < 2, z_own[f], z_high[f])
        return cells4, pltpu.roll(cells4, 127, 1), pltpu.roll(cells4, 126, 1), pltpu.roll(cells4, 125, 1)

    _, rho_left, rho_right, _ = z_last(9)
    _, mom_left, mom_right, _ = z_last(12)
    last_z = face_terms(rho_left, rho_right, mom_left, mom_right)
    for f in range(fields):
        y_rows[f, pl.ds(6, 8, stride=8), :] = y_low[f, 0]
        y_rows[f, pl.ds(7, 8, stride=8), :] = y_low[f, 1]
        y_rows[f, pl.ds(0, 8, stride=8), :] = y_high[f, 0]
        y_flux[f, pl.ds(7, 8, stride=8), :] = face_flux(
            last_y, diff[f], y_own[1, f, 0], y_own[1, f, 1], y_high[f, 0], y_high[f, 1]
        )
        z_flux[f] = face_flux(last_z, diff[f], *z_last(f))

    for x in range(8):
        _, rho_left, _ = shifted(tile(9, x), y_rows[9, pl.ds(8 * x, 8), :], line, 8, 0)
        _, mom_left, _ = shifted(tile(11, x), y_rows[11, pl.ds(8 * x, 8), :], line, 8, 0)
        found = face_terms(rho_left, tile(9, x), mom_left, tile(11, x))
        _, rho_left, _ = shifted(tile(9, x), z_next(9, x), lane, 128, 1)
        _, mom_left, _ = shifted(tile(12, x), z_next(12, x), lane, 128, 1)
        found = found + face_terms(rho_left, tile(9, x), mom_left, tile(12, x))
        for i in range(12):
            terms[x, i] = found[i]

    def along_yz(f, carry):
        for x in range(8):
            here = tile(f, x)
            rows = pl.ds(8 * x, 8)
            far_left, left, far_right = shifted(here, y_rows[f, rows, :], line, 8, 0)
            low = face_flux([terms[x, i] for i in range(6)], diff[f], far_left, left, here, far_right)
            high = jnp.where(line == 7, y_flux[f, rows, :], pltpu.roll(low, 7, 0))
            total = here + (low - high)
            far_left, left, far_right = shifted(here, z_next(f, x), lane, 128, 1)
            low = face_flux([terms[x, 6 + i] for i in range(6)], diff[f], far_left, left, here, far_right)
            last = pltpu.roll(z_flux[f], 127 - 4 * x, 1)
            high = jnp.where(lane == 127, last, pltpu.roll(low, 127, 1))
            out[f, rows, :] = total + (low - high)
        return carry

    lax.fori_loop(0, fields, along_yz, 0)

    halos[4].wait_recv()
    halos[5].wait_recv()

    @pl.when(is_end)
    def _():
        every = pltpu.make_async_remote_copy(
            src_ref=arrived.at[pl.ds(0, n_y - 1)], dst_ref=arrived.at[pl.ds(0, n_y - 1)],
            send_sem=second_send, recv_sem=second_recv,
            device_id=y_at(1), device_id_type=MESH,
        )
        every.wait_recv()
        by_slot = arrived[...].reshape(256, 128).T
        by_slot = jnp.concatenate([by_slot[SLOT * s : SLOT * (s + 1)] for s in range(3)], axis=1)
        face = jnp.dot(split3(by_slot), spread[...], preferred_element_type=jnp.float32)
        face = face[:SLOT] + face[SLOT : 2 * SLOT] + face[2 * SLOT :]
        for y in range(8):
            h = y // 2
            plane[SLOT * y : SLOT * (y + 1), :] = face[:, 128 * h : 128 * (h + 1)]
        for end, start in ((0, 0), (n_x - 1, 80)):

            @pl.when(a == end)
            def _():
                for f in range(fields):
                    ghost = plane[pl.ds(f, 8, stride=SLOT), :]
                    qx[f, pl.ds(start, 8), :] = ghost
                    qx[f, pl.ds(start + 8, 8), :] = ghost

        every.wait_send()

    for i in range(9):
        left, right = pl.ds(8 * i + 8, 8), pl.ds(8 * i + 16, 8)
        found = face_terms(qx[9, left, :], qx[9, right, :], qx[10, left, :], qx[10, right, :])
        for j in range(6):
            terms[i, j] = found[j]

    def along_x(f, carry):
        low = None
        for i in range(9):
            cells4 = [qx[f, pl.ds(8 * (i + j), 8), :] for j in range(4)]
            high = face_flux([terms[i, j] for j in range(6)], diff[f], *cells4)
            if i > 0:
                rows = pl.ds(8 * (i - 1), 8)
                out[f, rows, :] = out[f, rows, :] + (low - high)
            low = high
        return carry

    lax.fori_loop(0, fields, along_x, 0)

    for which in range(2):

        @pl.when(a != (0, n_x - 1)[which])
        def _():
            to_end(which).wait_send()

    for copy in halos:
        copy.wait_send()


def solution(mesh):
    n_x, n_y, n_z = (mesh.shape[name] for name in ("gx", "gy", "gz"))

    def on_device(fine_state, diffusivity, coarse_cells, copy_sources, copy_targets):
        fields, cells_x, cells_y, cells_z = fine_state.shape
        rows = cells_x * cells_y
        peers = n_x * n_y
        sources = jnp.transpose(copy_sources, (0, 1, 4, 2, 3)).reshape(3, 1, peers)
        targets = jnp.transpose(copy_targets, (0, 1, 4, 2, 3)).reshape(3, 1, peers)
        f32 = jnp.float32
        vmem = pltpu.VMEM
        anywhere = pl.BlockSpec(memory_space=pl.ANY)
        result = pl.pallas_call(
            functools.partial(kernel, n_x, n_y, n_z, fields),
            out_shape=jax.ShapeDtypeStruct((fields, rows, cells_z), f32),
            in_specs=[anywhere, pl.BlockSpec(memory_space=pltpu.SMEM), anywhere, anywhere, anywhere],
            out_specs=pl.BlockSpec(memory_space=pltpu.VMEM),
            scratch_shapes=[
                vmem((fields, rows + 32, cells_z), f32),
                vmem((2, fields, 2, 8, 128), f32),
                vmem((fields, 2, 8, 128), f32),
                vmem((fields, 2, 8, 128), f32),
                vmem((fields, rows, 128), f32),
                vmem((fields, rows, 128), f32),
                vmem((fields, 8, 128), f32),
                vmem((fields, 8, 128), f32),
                vmem((fields, 8, 128), f32),
                vmem((fields, 8, 128), f32),
                vmem((fields, 128), f32),
                vmem((3, 1, peers), jnp.int32),
                vmem((3, 1, peers), jnp.int32),
                vmem((2, n_y, 128), f32),
                vmem((n_x, n_y, 128), f32),
                vmem((8 * n_y, 128), f32),
                vmem((32, 8, 128), f32),
                vmem((256, 128), f32),
                vmem((768, 512), jnp.bfloat16),
                vmem((8 * SLOT, 128), f32),
                vmem((9, 12, 8, 128), f32),
                pltpu.SemaphoreType.DMA((4,)),
                pltpu.SemaphoreType.DMA((6,)),
                pltpu.SemaphoreType.DMA((6,)),
                pltpu.SemaphoreType.DMA((2,)),
                pltpu.SemaphoreType.DMA((n_x,)),
                pltpu.SemaphoreType.DMA,
                pltpu.SemaphoreType.DMA,
            ],
            compiler_params=pltpu.CompilerParams(
                collective_id=0, has_side_effects=True, vmem_limit_bytes=56 * 1024 * 1024
            ),
        )(fine_state.reshape(fields, rows, cells_z), diffusivity, coarse_cells, sources, targets)
        return result.reshape(fine_state.shape)

    return jax.shard_map(
        on_device,
        mesh=mesh,
        in_specs=(
            P(None, "gx", "gy", "gz"),
            P(),
            P(None, ("gx", "gy", "gz")),
            P("gx", "gy", "gz", None, None),
            P("gx", "gy", "gz", None, None),
        ),
        out_specs=P(None, "gx", "gy", "gz"),
        check_vma=False,
    )
```

time: 73.6 us -> 32.3 us (0.44)
  the two profiles are of different devices: /device:TPU:26 before, /device:TPU:1 now
where the time goes in v1:
time: 32.3 us; the launch traced here: 32.1 us
  Pallas kernels  30.3 us (94%)
  local copies, waits for them, and re-layouts  1.82 us (6%)
    pallas_call x1, Pallas kernels, on_device(): pl.pallas_call(functools.partial(kernel, n_x, n_y, n_z, fields), out_shap...  30.3 us
    unnamed x1, local copies, waits for them, and re-layouts  1.82 us

profile of v1, /device:TPU:1, one launch (start us, length us, event | category | flops | bytes accessed | tf_op | source)
XLA Modules:
  0.0 32.1 jit_solution(5788779486486606131)
XLA Ops:
  0.0 30.3 %shard_map.55 = f32[14,64,128]{2,1,0:T(8,128)} custom-call(f32[14,64,128]{2,1,0:T(8,128)} %bitcast.9, f32[14]{0:T(128)} %diff.1, f32[14,128]{1,0:T(8,128)} %coarse.1, s32[3,1,96]{2,1,0:T(1,128)} %bitcast.10, s32[3,1,96]{2,1,0:T(1,128)} %bitcast.11), custom_call_target="tpu_custom_call" | custom-call | tf_op jit(solution)/shard_map/pallas_call | solution.py:342
  30.3 1.8 %copy.7 = f32[14,8,8,128]{3,2,1,0:T(8,128)} copy(f32[14,8,8,128]{3,2,1,0:T(8,128)} %bitcast.8) | data formatting | bytes 917504

commit v2 on v0

v2 whole, which is shorter than its diff:
```python
import functools

import jax
import jax.numpy as jnp
from jax import lax
from jax.experimental import pallas as pl
from jax.experimental.pallas import tpu as pltpu
from jax.sharding import PartitionSpec as P

MESH = pl.DeviceIdType.MESH
time_step = 0.15
SLOT = 16


def hubs_of(n_y):
    n_hubs = max(1, n_y // 4)
    return n_hubs, n_y // n_hubs


def split3(value):
    hi = value.astype(jnp.bfloat16)
    rest = value - hi.astype(jnp.float32)
    mid = rest.astype(jnp.bfloat16)
    low = (rest - mid.astype(jnp.float32)).astype(jnp.bfloat16)
    return jnp.concatenate([hi, mid, low], axis=0)


def face_terms(rho_left, rho_right, mom_left, mom_right):
    inv_left, inv_right = 1.0 / rho_left, 1.0 / rho_right
    velocity = (0.5 * time_step) * (mom_left * inv_left + mom_right * inv_right)
    up, down = jnp.maximum(velocity, 0.0), jnp.minimum(velocity, 0.0)
    quarter_up, quarter_down = 0.25 * up, 0.25 * down
    mean_rho = (0.5 * time_step) * (rho_left + rho_right)
    return (
        up + quarter_down,
        down + quarter_up,
        quarter_up,
        quarter_down,
        mean_rho * inv_left,
        mean_rho * inv_right,
    )


def cell_terms(low, high):
    a_left, a_right, b_left, b_right, e_left, e_right = low
    next_left, next_right, next_b_left, next_b_right, next_e_left, next_e_right = high
    around = (
        -b_left,
        a_left + next_b_left,
        e_left,
        -(b_right + next_right),
        next_e_right,
        next_b_right,
    )
    return around, (a_right - next_left, -(e_right + next_e_left))


def weighted(found, diff, far_low, low, high, far_high):
    w_far_low, w_low, d_low, w_high, d_high, w_far_high = found
    return (
        (w_far_low * far_low + w_far_high * far_high)
        + (w_low + diff * d_low) * low
        + (w_high + diff * d_high) * high
    )


def work(n_x, n_y, fields, diff, out, qx, y_own, y_low, y_high, y_pad, z_own, z_low, z_high, z_rows,
         cells, src, tgt, msg, relay, arrived, order, spread, plane, terms):
    peers = n_x * n_y
    n_hubs, per_hub = hubs_of(n_y)
    lane = lax.broadcasted_iota(jnp.int32, (8, 128), 1)
    line = lax.broadcasted_iota(jnp.int32, (8, 128), 0)
    blank = jnp.full((1, 128 - peers), -1, jnp.int32)

    def pick():
        owned = jnp.concatenate([cells[...], jnp.zeros((SLOT - fields, 128), jnp.float32)], axis=0)
        owned = split3(owned)
        row = lax.broadcasted_iota(jnp.int32, (128, 128), 0)
        picked = []
        for s in range(3):
            wanted = jnp.concatenate([src[s], blank], axis=1)
            chosen = jnp.where(row == wanted, 1.0, 0.0).astype(jnp.bfloat16)
            part = jnp.dot(owned, chosen, preferred_element_type=jnp.float32)
            picked.append(part[:SLOT] + part[SLOT : 2 * SLOT] + part[2 * SLOT :])
        picked.append(jnp.zeros((128 - 3 * SLOT, 128), jnp.float32))
        picked = jnp.concatenate(picked, axis=0).T
        n_early = n_y // 2
        for which, start in enumerate((0, peers - n_y)):
            msg[which, : n_y - n_early] = picked[start + n_early : start + n_y].reshape(n_y - n_early, 1, 128)
            msg[which, n_y - n_early :] = picked[start : start + n_early].reshape(n_early, 1, 128)

    def pack():
        for f in range(fields):
            y_own[0, f, 0] = qx[f, pl.ds(16, 8, stride=8), :]
            y_own[0, f, 1] = qx[f, pl.ds(17, 8, stride=8), :]
            y_own[1, f, 0] = qx[f, pl.ds(22, 8, stride=8), :]
            y_own[1, f, 1] = qx[f, pl.ds(23, 8, stride=8), :]
            packed = pltpu.roll(qx[f, pl.ds(16, 8), :], 2, 1)
            for x in range(1, 8):
                moved = pltpu.roll(qx[f, pl.ds(16 + 8 * x, 8), :], 4 * x + 2, 1)
                packed = jnp.where(lane >= 4 * x, moved, packed)
            z_own[f] = packed

    def pad():
        for f in range(fields):
            for x in range(8):
                y_pad[f, pl.ds(16 * x + 8, 8), :] = tile(f, x)

    def place():
        wide = [jnp.concatenate([tgt[s], blank], axis=1) for s in range(3)]
        wide.append(jnp.full((125, 128), -1, jnp.int32))
        wide = jnp.concatenate(wide, axis=0).astype(jnp.float32).T
        order[...] = jnp.full(order.shape, -1.0, jnp.float32)
        count = n_x * per_hub
        for a in range(n_x):
            for k in range(per_hub):
                start = a * n_y + k * n_hubs
                order[pl.ds(a * per_hub + k, n_hubs, stride=count), :] = wide[start : start + n_hubs]
        half = (lax.broadcasted_iota(jnp.int32, (128, 128), 1) // 2).astype(jnp.float32)
        filled = order[...]
        for s in range(3):
            cell = filled[:, s : s + 1]
            for h in range(4):
                spread[128 * s : 128 * (s + 1), 128 * h : 128 * (h + 1)] = jnp.where(
                    cell - 64.0 * h == half, 1.0, 0.0
                ).astype(jnp.bfloat16)
        if peers < 128:
            arrived[peers:] = jnp.zeros((128 - peers, 1, 128), jnp.float32)

    def tile(f, x):
        return qx[f, pl.ds(16 + 8 * x, 8), :]

    def spread_halos():
        for f in range(fields):
            y_pad[f, pl.ds(6, 8, stride=16), :] = y_low[f, 0]
            y_pad[f, pl.ds(7, 8, stride=16), :] = y_low[f, 1]
            y_pad[f, pl.ds(16, 8, stride=16), :] = y_high[f, 0]
            y_pad[f, pl.ds(17, 8, stride=16), :] = y_high[f, 1]
            kept = jnp.where(lane % 4 < 2, z_low[f], z_high[f])
            for x in range(8):
                z_rows[f, pl.ds(8 * x, 8), :] = pltpu.roll(kept, 126 - 4 * x, 1)

    def y_at(f, x, k):
        return y_pad[f, pl.ds(16 * x + 8 + k, 8), :]

    def x_at(f, x, k):
        return qx[f, pl.ds(8 * (x + k) + 16, 8), :]

    def z_all(f, x, here):
        beyond = z_rows[f, pl.ds(8 * x, 8), :]
        return (
            pltpu.roll(jnp.where(lane >= 126, beyond, here), 2, 1),
            pltpu.roll(jnp.where(lane == 127, beyond, here), 1, 1),
            pltpu.roll(jnp.where(lane == 0, beyond, here), 127, 1),
            pltpu.roll(jnp.where(lane < 2, beyond, here), 126, 1),
        )

    def three(rho, mom):
        low = face_terms(rho[0], rho[1], mom[0], mom[1])
        high = face_terms(rho[1], rho[2], mom[1], mom[2])
        return cell_terms(low, high)

    def x_terms(x):
        return three([x_at(9, x, k) for k in (-1, 0, 1)], [x_at(10, x, k) for k in (-1, 0, 1)])

    def cell_weights():
        for x in range(8):
            found, (centre, d_centre) = three([y_at(9, x, k) for k in (-1, 0, 1)], [y_at(11, x, k) for k in (-1, 0, 1)])
            rho, mom = tile(9, x), tile(12, x)
            _, rho_low, rho_high, _ = z_all(9, x, rho)
            _, mom_low, mom_high, _ = z_all(12, x, mom)
            more, (c, d) = three([rho_low, rho, rho_high], [mom_low, mom, mom_high])
            found, centre, d_centre = found + more, centre + c, d_centre + d
            if 2 <= x < 6:
                more, (c, d) = x_terms(x)
                found, centre, d_centre = found + more, centre + c, d_centre + d
            found = found + (1.0 + centre, d_centre)
            for i, value in enumerate(found):
                terms[x, i] = value

    def main_flux():
        def one_field(g, carry):
            for x in range(8):
                for f in (2 * g, 2 * g + 1):
                    here = tile(f, x)
                    inner = 2 <= x < 6
                    found = [terms[x, i] for i in range(20 if inner else 14)]
                    total = here * (found[-2] + diff[f] * found[-1])
                    total = total + weighted(found[:6], diff[f], *[y_at(f, x, k) for k in (-2, -1, 1, 2)])
                    if inner:
                        total = total + weighted(found[12:18], diff[f], *[x_at(f, x, k) for k in (-2, -1, 1, 2)])
                    total = total + weighted(found[6:12], diff[f], *z_all(f, x, here))
                    out[f, pl.ds(8 * x, 8), :] = total
            return carry

        lax.fori_loop(0, fields // 2, one_field, 0)

    def edge_flux(first_x):
        kept = []
        for x in (first_x, first_x + 1):
            found, centre = x_terms(x)
            kept.append(found + centre)
        for f in range(fields):
            for x, found in zip((first_x, first_x + 1), kept):
                rows = pl.ds(8 * x, 8)
                total = tile(f, x) * (found[-2] + diff[f] * found[-1])
                total = total + weighted(found[:6], diff[f], *[x_at(f, x, k) for k in (-2, -1, 1, 2)])
                out[f, rows, :] = out[f, rows, :] + total

    def ghost():
        by_slot = arrived[...].reshape(128, 128).T
        by_slot = jnp.concatenate([by_slot[SLOT * s : SLOT * (s + 1)] for s in range(3)], axis=1)
        face = jnp.dot(split3(by_slot), spread[...], preferred_element_type=jnp.float32)
        face = face[:SLOT] + face[SLOT : 2 * SLOT] + face[2 * SLOT :]
        for y in range(8):
            h = y // 2
            plane[SLOT * y : SLOT * (y + 1), :] = face[:, 128 * h : 128 * (h + 1)]

    def use_ghost(start):
        for f in range(fields):
            cover = plane[pl.ds(f, 8, stride=SLOT), :]
            qx[f, pl.ds(start, 8), :] = cover
            qx[f, pl.ds(start + 8, 8), :] = cover

    return dict(
        pick=pick, pack=pack, pad=pad, place=place, spread_halos=spread_halos, cell_weights=cell_weights,
        main_flux=main_flux, ghost=ghost, use_ghost=use_ghost, edge_flux=edge_flux,
    )


def kernel(
    n_x, n_y, n_z, fields,
    fine, diff, coarse, sources, targets,
    out,
    qx, y_own, y_low, y_high, y_pad, z_own, z_low, z_high, z_rows,
    cells, src, tgt, msg, relay, arrived, order, spread, plane, terms,
    load_sem, halo_send, halo_recv, row_send, row_recv, block_send, block_recv, pass_send, pass_recv, ready,
):
    a, b, c = lax.axis_index("gx"), lax.axis_index("gy"), lax.axis_index("gz")
    is_end = jnp.logical_or(a == 0, a == n_x - 1)
    peers = n_x * n_y
    n_hubs, per_hub = hubs_of(n_y)
    served = n_x * per_hub
    step = work(
        n_x, n_y, fields, diff, out, qx, y_own, y_low, y_high, y_pad, z_own, z_low, z_high, z_rows,
        cells, src, tgt, msg, relay, arrived, order, spread, plane, terms,
    )

    n_early = n_y // 2
    ends = (0, n_x - 1)
    corner = jnp.logical_and(jnp.logical_and(a == 0, b == 0), c == 0)
    is_first = jnp.logical_and(jnp.logical_and(is_end, b < n_early), jnp.logical_not(corner))
    is_hub = jnp.logical_and(jnp.logical_and(is_end, b < n_early), b >= n_early - n_hubs)
    is_late = jnp.logical_and(is_end, jnp.logical_not(is_first))
    with_corner = c == 0
    n_late = n_y - n_early
    row = lax.rem(b, n_hubs) * served + a * per_hub + lax.div(b, n_hubs)

    def x_at(k):
        return (lax.rem(a + (k + n_x), n_x), b, c)

    def y_at(k):
        return (a, lax.rem(b + (k + n_y), n_y), c)

    def z_at(k):
        return (a, b, lax.rem(c + (k + n_z), n_z))

    load_cells = pltpu.make_async_copy(coarse, cells, load_sem.at[0])
    load_src = pltpu.make_async_copy(sources, src, load_sem.at[1])
    load_fine = pltpu.make_async_copy(fine, qx.at[:, pl.ds(16, 64)], load_sem.at[2])
    load_tgt = pltpu.make_async_copy(targets, tgt, load_sem.at[3])
    load_cells.start()
    load_src.start()
    load_fine.start()
    load_tgt.start()

    barrier = pltpu.get_barrier_semaphore()

    def greet(device):
        pl.semaphore_signal(barrier, inc=1, device_id=device, device_id_type=MESH)

    for k in (1, -1):
        greet(x_at(k))
        greet(y_at(k))
        greet(z_at(k))

    @pl.when(is_first)
    def _():
        for k in range(n_x):
            for peer in range(n_y):

                @pl.when(jnp.logical_or(a != k, b != peer))
                def _():
                    greet((k, peer, c))

    load_cells.wait()
    load_src.wait()
    step["pick"]()
    pl.semaphore_wait(barrier, 6 + 2 * n_early - jnp.where(with_corner, 1, 0) - jnp.where(is_first, 1, 0))

    def to_first(which, peer):
        return pltpu.make_async_remote_copy(
            src_ref=msg.at[which, pl.ds(n_late + peer, 1)], dst_ref=arrived.at[pl.ds(row, 1)],
            send_sem=row_send, recv_sem=row_recv,
            device_id=(ends[which], peer, c), device_id_type=MESH,
        )

    def to_hub(which):
        slot = a * per_hub + lax.div(b, n_hubs)
        return pltpu.make_async_remote_copy(
            src_ref=msg.at[which, pl.ds(0, n_late + 1)], dst_ref=relay.at[slot],
            send_sem=block_send.at[which], recv_sem=block_recv,
            device_id=(ends[which], n_early - n_hubs + lax.rem(b, n_hubs), c), device_id_type=MESH,
        )

    for peer in range(n_early):
        for which in range(2):
            itself = jnp.logical_and(a == ends[which], b == peer)
            meant = jnp.logical_not(itself)
            if peer == 0 and which == 0:
                meant = jnp.logical_and(meant, jnp.logical_not(with_corner))
                itself = jnp.logical_and(itself, jnp.logical_not(with_corner))

            @pl.when(meant)
            def _():
                to_first(which, peer).start()

            @pl.when(itself)
            def _():
                arrived[pl.ds(row, 1)] = msg[which, pl.ds(n_late + peer, 1)]

    def own_hub(which):
        return jnp.logical_and(a == ends[which], b == n_early - n_hubs + lax.rem(b, n_hubs))

    for which in range(2):

        @pl.when(jnp.logical_not(own_hub(which)))
        def _():
            to_hub(which).start()

        @pl.when(own_hub(which))
        def _():
            relay[a * per_hub + lax.div(b, n_hubs)] = msg[which, pl.ds(0, n_late + 1)]

    @pl.when(is_late)
    def _():
        for h in range(n_hubs):
            pl.semaphore_signal(ready, inc=1, device_id=(a, n_early - n_hubs + h, c), device_id_type=MESH)

    def halo(i, source, target, device):
        return pltpu.make_async_remote_copy(
            src_ref=source, dst_ref=target, send_sem=halo_send.at[i], recv_sem=halo_recv.at[i],
            device_id=device, device_id_type=MESH,
        )

    load_fine.wait()
    step["pack"]()
    to_low = halo(4, qx.at[:, pl.ds(16, 16)], qx.at[:, pl.ds(80, 16)], x_at(-1))
    to_high = halo(5, qx.at[:, pl.ds(64, 16)], qx.at[:, pl.ds(0, 16)], x_at(1))
    has_low, has_high = a > 0, a < n_x - 1
    halos = [
        halo(1, y_own.at[1], y_low, y_at(1)),
        halo(0, y_own.at[0], y_high, y_at(-1)),
        halo(2, z_own, z_high, z_at(-1)),
        halo(3, z_own, z_low, z_at(1)),
    ]
    for copy in halos:
        copy.start()

    @pl.when(has_low)
    def _():
        to_low.start()

    @pl.when(has_high)
    def _():
        to_high.start()

    load_tgt.wait()

    @pl.when(is_end)
    def _():
        step["place"]()

    step["pad"]()
    for copy in halos:
        copy.wait_recv()
    step["spread_halos"]()
    step["cell_weights"]()
    step["main_flux"]()

    @pl.when(has_high)
    def _():
        to_low.wait_recv()
        step["edge_flux"](6)

    @pl.when(has_low)
    def _():
        to_high.wait_recv()
        step["edge_flux"](0)

    def to_late(peer):
        return pltpu.make_async_remote_copy(
            src_ref=relay.at[:, (peer - n_early) % n_y],
            dst_ref=arrived.at[pl.ds((b - (n_early - n_hubs)) * served, served)],
            send_sem=pass_send, recv_sem=pass_recv,
            device_id=(a, peer, c), device_id_type=MESH,
        )

    def rows_of(count, send, recv):
        rows = arrived.at[pl.ds(0, count)]
        return pltpu.make_async_remote_copy(
            src_ref=rows, dst_ref=rows, send_sem=send, recv_sem=recv, device_id=y_at(1), device_id_type=MESH
        )

    has_corner = jnp.logical_and(with_corner, a == 0)

    @pl.when(is_hub)
    def _():
        blocks = relay.at[pl.ds(0, served - 1)]
        pltpu.make_async_remote_copy(
            src_ref=blocks, dst_ref=blocks, send_sem=block_send.at[0], recv_sem=block_recv,
            device_id=y_at(1), device_id_type=MESH,
        ).wait_recv()
        pl.semaphore_wait(ready, n_late + jnp.where(has_corner, 1, 0))
        for peer in range(n_early, n_y):
            to_late(peer).start()

        @pl.when(has_corner)
        def _():
            to_late(0).start()

    @pl.when(is_first)
    def _():
        rows_of(peers - 1, row_send, row_recv).wait_recv()

    @pl.when(is_late)
    def _():
        rows_of(peers, pass_send, pass_recv).wait_recv()

    @pl.when(is_end)
    def _():
        step["ghost"]()
        for end, start, first_x in ((0, 0, 0), (n_x - 1, 80, 6)):

            @pl.when(a == end)
            def _():
                step["use_ghost"](start)
                step["edge_flux"](first_x)

    @pl.when(is_hub)
    def _():
        for _ in range(n_late * served // peers):
            rows_of(peers, pass_send, pass_recv).wait_send()

        @pl.when(has_corner)
        def _():
            rows_of(served, pass_send, pass_recv).wait_send()

    rows_of(2 * n_early - 2, row_send, row_recv).wait_send()

    @pl.when(jnp.logical_not(is_first))
    def _():
        rows_of(1, row_send, row_recv).wait_send()

    @pl.when(jnp.logical_not(with_corner))
    def _():
        rows_of(1, row_send, row_recv).wait_send()

    for which in range(2):

        @pl.when(jnp.logical_not(own_hub(which)))
        def _():
            to_hub(which).wait_send()

    for copy in halos:
        copy.wait_send()

    @pl.when(has_low)
    def _():
        to_low.wait_send()

    @pl.when(has_high)
    def _():
        to_high.wait_send()


def solution(mesh):
    n_x, n_y, n_z = (mesh.shape[name] for name in ("gx", "gy", "gz"))

    def on_device(fine_state, diffusivity, coarse_cells, copy_sources, copy_targets):
        fields, cells_x, cells_y, cells_z = fine_state.shape
        rows = cells_x * cells_y
        peers = n_x * n_y
        n_hubs, per_hub = hubs_of(n_y)
        sources = jnp.transpose(copy_sources, (0, 1, 4, 2, 3)).reshape(3, 1, peers)
        targets = jnp.transpose(copy_targets, (0, 1, 4, 2, 3)).reshape(3, 1, peers)
        f32 = jnp.float32
        vmem = pltpu.VMEM
        anywhere = pl.BlockSpec(memory_space=pl.ANY)
        result = pl.pallas_call(
            functools.partial(kernel, n_x, n_y, n_z, fields),
            out_shape=jax.ShapeDtypeStruct((fields, rows, cells_z), f32),
            in_specs=[anywhere, pl.BlockSpec(memory_space=pltpu.SMEM), anywhere, anywhere, anywhere],
            out_specs=pl.BlockSpec(memory_space=pltpu.VMEM),
            scratch_shapes=[
                vmem((fields, rows + 32, cells_z), f32),
                vmem((2, fields, 2, 8, 128), f32),
                vmem((fields, 2, 8, 128), f32),
                vmem((fields, 2, 8, 128), f32),
                vmem((fields, 16 * 8 + 16, 128), f32),
                vmem((fields, 8, 128), f32),
                vmem((fields, 8, 128), f32),
                vmem((fields, 8, 128), f32),
                vmem((fields, rows, 128), f32),
                vmem((fields, 128), f32),
                vmem((3, 1, peers), jnp.int32),
                vmem((3, 1, peers), jnp.int32),
                vmem((2, n_y, 1, 128), f32),
                vmem((n_x * per_hub, n_y - n_y // 2 + 1, 1, 128), f32),
                vmem((128, 1, 128), f32),
                vmem((128, 128), f32),
                vmem((384, 512), jnp.bfloat16),
                vmem((8 * SLOT, 128), f32),
                vmem((8, 20, 8, 128), f32),
                pltpu.SemaphoreType.DMA((4,)),
                pltpu.SemaphoreType.DMA((6,)),
                pltpu.SemaphoreType.DMA((6,)),
                pltpu.SemaphoreType.DMA,
                pltpu.SemaphoreType.DMA,
                pltpu.SemaphoreType.DMA((2,)),
                pltpu.SemaphoreType.DMA,
                pltpu.SemaphoreType.DMA,
                pltpu.SemaphoreType.DMA,
                pltpu.SemaphoreType.REGULAR,
            ],
            compiler_params=pltpu.CompilerParams(
                collective_id=0, has_side_effects=True, vmem_limit_bytes=56 * 1024 * 1024
            ),
        )(fine_state.reshape(fields, rows, cells_z), diffusivity, coarse_cells, sources, targets)
        return result.reshape(fine_state.shape)

    return jax.shard_map(
        on_device,
        mesh=mesh,
        in_specs=(
            P(None, "gx", "gy", "gz"),
            P(),
            P(None, ("gx", "gy", "gz")),
            P("gx", "gy", "gz", None, None),
            P("gx", "gy", "gz", None, None),
        ),
        out_specs=P(None, "gx", "gy", "gz"),
        check_vma=False,
    )
```

time: 73.6 us -> 26.9 us (0.37)
  the two profiles are of different devices: /device:TPU:26 before, /device:TPU:1 now
where the time goes in v2:
time: 26.9 us; the launch traced here: 26.7 us
  Pallas kernels  24.9 us (93%)
  local copies, waits for them, and re-layouts  1.82 us (7%)
    pallas_call x1, Pallas kernels, on_device(): pl.pallas_call(functools.partial(kernel, n_x, n_y, n_z, fields), out_shap...  24.9 us
    unnamed x1, local copies, waits for them, and re-layouts  1.82 us

profile of v2, /device:TPU:1, one launch (start us, length us, event | category | flops | bytes accessed | tf_op | source)
XLA Modules:
  0.0 26.7 jit_solution(3136947034310913541)
XLA Ops:
  0.0 24.9 %shard_map.55 = f32[14,64,128]{2,1,0:T(8,128)} custom-call(f32[14,64,128]{2,1,0:T(8,128)} %bitcast.9, f32[14]{0:T(128)} %diff.1, f32[14,128]{1,0:T(8,128)} %coarse.1, s32[3,1,96]{2,1,0:T(1,128)} %bitcast.10, s32[3,1,96]{2,1,0:T(1,128)} %bitcast.11), custom_call_target="tpu_custom_call" | custom-call | tf_op jit(solution)/shard_map/pallas_call | solution.py:500
  24.9 1.8 %copy.7 = f32[14,8,8,128]{3,2,1,0:T(8,128)} copy(f32[14,8,8,128]{3,2,1,0:T(8,128)} %bitcast.8) | data formatting | bytes 917504

commit v3 on v2

--- a/solution.py
+++ b/solution.py
@@ -234,7 +234,7 @@
     out,
     qx, y_own, y_low, y_high, y_pad, z_own, z_low, z_high, z_rows,
     cells, src, tgt, msg, relay, arrived, order, spread, plane, terms,
-    load_sem, halo_send, halo_recv, row_send, row_recv, block_send, block_recv, pass_send, pass_recv, ready,
+    load_sem, halo_send, halo_recv, row_send, row_recv, block_send, block_recv, pass_send, pass_recv, ready, open_sem,
 ):
     a, b, c = lax.axis_index("gx"), lax.axis_index("gy"), lax.axis_index("gz")
     is_end = jnp.logical_or(a == 0, a == n_x - 1)
@@ -279,10 +279,23 @@
     def greet(device):
         pl.semaphore_signal(barrier, inc=1, device_id=device, device_id_type=MESH)
 
-    for k in (1, -1):
-        greet(x_at(k))
-        greet(y_at(k))
-        greet(z_at(k))
+    has_low, has_high = a > 0, a < n_x - 1
+    y_later = (b < n_y - 1, b == 0)
+    z_later = (c < n_z // 2, jnp.logical_or(c == 0, c > n_z // 2))
+    neighbours = [
+        (y_at(1), y_later[0], jnp.logical_not(y_later[0]), 1),
+        (y_at(-1), y_later[1], jnp.logical_not(y_later[1]), 0),
+        (z_at(1), z_later[0], jnp.logical_not(z_later[0]), 3),
+        (z_at(-1), z_later[1], jnp.logical_not(z_later[1]), 2),
+        (x_at(1), has_high, False, 5),
+        (x_at(-1), False, has_low, 4),
+    ]
+    n_earlier = 0
+    for device, later, earlier, _ in neighbours:
+        if later is not False:
+            pl.when(later)(functools.partial(greet, device))
+        if earlier is not False:
+            n_earlier = n_earlier + jnp.where(earlier, 1, 0)
 
     @pl.when(is_first)
     def _():
@@ -296,7 +309,14 @@
     load_cells.wait()
     load_src.wait()
     step["pick"]()
-    pl.semaphore_wait(barrier, 6 + 2 * n_early - jnp.where(with_corner, 1, 0) - jnp.where(is_first, 1, 0))
+    pl.semaphore_wait(barrier, n_earlier + 2 * n_early - jnp.where(with_corner, 1, 0) - jnp.where(is_first, 1, 0))
+
+    def tell(device, number):
+        pl.semaphore_signal(open_sem.at[number], inc=1, device_id=device, device_id_type=MESH)
+
+    for device, _, earlier, number in neighbours:
+        if earlier is not False:
+            pl.when(earlier)(functools.partial(tell, device, number))
 
     def to_first(which, peer):
         return pltpu.make_async_remote_copy(
@@ -355,26 +375,28 @@
 
     load_fine.wait()
     step["pack"]()
-    to_low = halo(4, qx.at[:, pl.ds(16, 16)], qx.at[:, pl.ds(80, 16)], x_at(-1))
-    to_high = halo(5, qx.at[:, pl.ds(64, 16)], qx.at[:, pl.ds(0, 16)], x_at(1))
-    has_low, has_high = a > 0, a < n_x - 1
     halos = [
-        halo(1, y_own.at[1], y_low, y_at(1)),
-        halo(0, y_own.at[0], y_high, y_at(-1)),
-        halo(2, z_own, z_high, z_at(-1)),
-        halo(3, z_own, z_low, z_at(1)),
+        halo(0, y_own.at[1], y_low, y_at(1)),
+        halo(1, y_own.at[0], y_high, y_at(-1)),
+        halo(2, z_own, z_low, z_at(1)),
+        halo(3, z_own, z_high, z_at(-1)),
+        halo(4, qx.at[:, pl.ds(64, 16)], qx.at[:, pl.ds(0, 16)], x_at(1)),
+        halo(5, qx.at[:, pl.ds(16, 16)], qx.at[:, pl.ds(80, 16)], x_at(-1)),
     ]
-    for copy in halos:
-        copy.start()
-
-    @pl.when(has_low)
-    def _():
-        to_low.start()
-
-    @pl.when(has_high)
-    def _():
-        to_high.start()
-
+    to_high, to_low = halos[4:]
+
+    def send_later(i):
+        pl.semaphore_wait(open_sem.at[i], 1)
+        halos[i].start()
+
+    for i, (_, _, earlier, _) in enumerate(neighbours):
+        if earlier is not False:
+            pl.when(earlier)(halos[i].start)
+    for i in (5, 4, 3, 2, 0, 1):
+        later = neighbours[i][1]
+        if later is not False:
+            pl.when(later)(functools.partial(send_later, i))
+    halos = halos[:4]
     load_tgt.wait()
 
     @pl.when(is_end)
@@ -499,7 +521,7 @@
         anywhere = pl.BlockSpec(memory_space=pl.ANY)
         result = pl.pallas_call(
             functools.partial(kernel, n_x, n_y, n_z, fields),
-            out_shape=jax.ShapeDtypeStruct((fields, rows, cells_z), f32),
+            out_shape=pltpu.VMEM((fields, rows, cells_z), f32),
             in_specs=[anywhere, pl.BlockSpec(memory_space=pltpu.SMEM), anywhere, anywhere, anywhere],
             out_specs=pl.BlockSpec(memory_space=pltpu.VMEM),
             scratch_shapes=[
@@ -532,6 +554,7 @@
                 pltpu.SemaphoreType.DMA,
                 pltpu.SemaphoreType.DMA,
                 pltpu.SemaphoreType.REGULAR,
+                pltpu.SemaphoreType.REGULAR((6,)),
             ],
             compiler_params=pltpu.CompilerParams(
                 collective_id=0, has_side_effects=True, vmem_limit_bytes=56 * 1024 * 1024

time: 26.9 us -> 24.1 us (0.90)
  Pallas kernels: 24.9 us -> 23.2 us
  local copies, waits for them, and re-layouts: 1.82 us -> 0.77 us
    pallas_call x1, Pallas kernels: 24.9 us -> 23.2 us  [on_device(): pl.pallas_call(functools.partial(kernel, n_x, n_y, n_z, fields), out_shap...]
    unnamed x1, local copies, waits for them, and re-layouts: 1.82 us -> 0.77 us
where the time goes in v3:
time: 24.1 us; the launch traced here: 23.9 us
  Pallas kernels  23.2 us (96%)
  local copies, waits for them, and re-layouts  0.77 us (3%)
    pallas_call x1, Pallas kernels, on_device(): pl.pallas_call(functools.partial(kernel, n_x, n_y, n_z, fields), out_shap...  23.2 us
    unnamed x1, local copies, waits for them, and re-layouts  0.77 us

profile of v3, /device:TPU:1, one launch (start us, length us, event | category | flops | bytes accessed | tf_op | source)
XLA Modules:
  0.0 23.9 jit_solution(15249197554582323454)
XLA Ops:
  0.0 23.2 %shard_map.55 = f32[14,64,128]{2,1,0:T(8,128)S(1)} custom-call(f32[14,64,128]{2,1,0:T(8,128)} %bitcast.9, f32[14]{0:T(128)} %diff.1, f32[14,128]{1,0:T(8,128)} %coarse.1, s32[3,1,96]{2,1,0:T(1,128)} %bitcast.10, s32[3,1,96]{2,1,0:T(1,128)} %bitcast.11), custom_call_target="tpu_custom_call" | custom-call | tf_op jit(solution)/shard_map/pallas_call | solution.py:522
  23.2 0.8 %copy.7 = f32[14,8,8,128]{3,2,1,0:T(8,128)} copy(f32[14,8,8,128]{3,2,1,0:T(8,128)S(1)} %bitcast.8) | data formatting | bytes 917504

commit v4 on v3

--- a/solution.py
+++ b/solution.py
@@ -15,6 +15,10 @@
 def hubs_of(n_y):
     n_hubs = max(1, n_y // 4)
     return n_hubs, n_y // n_hubs
+
+
+def early_of(n_y):
+    return max(2, 5 * n_y // 12)
 
 
 def split3(value):
@@ -84,7 +88,7 @@
             picked.append(part[:SLOT] + part[SLOT : 2 * SLOT] + part[2 * SLOT :])
         picked.append(jnp.zeros((128 - 3 * SLOT, 128), jnp.float32))
         picked = jnp.concatenate(picked, axis=0).T
-        n_early = n_y // 2
+        n_early = early_of(n_y)
         for which, start in enumerate((0, peers - n_y)):
             msg[which, : n_y - n_early] = picked[start + n_early : start + n_y].reshape(n_y - n_early, 1, 128)
             msg[which, n_y - n_early :] = picked[start : start + n_early].reshape(n_early, 1, 128)
@@ -130,15 +134,18 @@
     def tile(f, x):
         return qx[f, pl.ds(16 + 8 * x, 8), :]
 
-    def spread_halos():
+    def spread_z():
+        for f in range(fields):
+            kept = jnp.where(lane % 4 < 2, z_low[f], z_high[f])
+            for x in range(8):
+                z_rows[f, pl.ds(8 * x, 8), :] = pltpu.roll(kept, 126 - 4 * x, 1)
+
+    def spread_y():
         for f in range(fields):
             y_pad[f, pl.ds(6, 8, stride=16), :] = y_low[f, 0]
             y_pad[f, pl.ds(7, 8, stride=16), :] = y_low[f, 1]
             y_pad[f, pl.ds(16, 8, stride=16), :] = y_high[f, 0]
             y_pad[f, pl.ds(17, 8, stride=16), :] = y_high[f, 1]
-            kept = jnp.where(lane % 4 < 2, z_low[f], z_high[f])
-            for x in range(8):
-                z_rows[f, pl.ds(8 * x, 8), :] = pltpu.roll(kept, 126 - 4 * x, 1)
 
     def y_at(f, x, k):
         return y_pad[f, pl.ds(16 * x + 8 + k, 8), :]
@@ -163,37 +170,53 @@
     def x_terms(x):
         return three([x_at(9, x, k) for k in (-1, 0, 1)], [x_at(10, x, k) for k in (-1, 0, 1)])
 
-    def cell_weights():
+    def store_terms(x, first, found):
+        for i, value in enumerate(found):
+            terms[x, first + i] = value
+
+    def weights_zx():
         for x in range(8):
-            found, (centre, d_centre) = three([y_at(9, x, k) for k in (-1, 0, 1)], [y_at(11, x, k) for k in (-1, 0, 1)])
             rho, mom = tile(9, x), tile(12, x)
             _, rho_low, rho_high, _ = z_all(9, x, rho)
             _, mom_low, mom_high, _ = z_all(12, x, mom)
-            more, (c, d) = three([rho_low, rho, rho_high], [mom_low, mom, mom_high])
-            found, centre, d_centre = found + more, centre + c, d_centre + d
+            found, (centre, d_centre) = three([rho_low, rho, rho_high], [mom_low, mom, mom_high])
             if 2 <= x < 6:
                 more, (c, d) = x_terms(x)
                 found, centre, d_centre = found + more, centre + c, d_centre + d
-            found = found + (1.0 + centre, d_centre)
-            for i, value in enumerate(found):
-                terms[x, i] = value
-
-    def main_flux():
-        def one_field(g, carry):
+            store_terms(x, 0, found + (1.0 + centre, d_centre))
+
+    def weights_y():
+        for x in range(8):
+            found, centre = three([y_at(9, x, k) for k in (-1, 0, 1)], [y_at(11, x, k) for k in (-1, 0, 1)])
+            store_terms(x, 14, found + centre)
+
+    def flux_zx():
+        def two_fields(g, carry):
             for x in range(8):
                 for f in (2 * g, 2 * g + 1):
                     here = tile(f, x)
                     inner = 2 <= x < 6
-                    found = [terms[x, i] for i in range(20 if inner else 14)]
+                    found = [terms[x, i] for i in range(14 if inner else 8)]
                     total = here * (found[-2] + diff[f] * found[-1])
+                    if inner:
+                        total = total + weighted(found[6:12], diff[f], *[x_at(f, x, k) for k in (-2, -1, 1, 2)])
+                    out[f, pl.ds(8 * x, 8), :] = total + weighted(found[:6], diff[f], *z_all(f, x, here))
+            return carry
+
+        lax.fori_loop(0, fields // 2, two_fields, 0)
+
+    def flux_y():
+        def two_fields(g, carry):
+            for x in range(8):
+                for f in (2 * g, 2 * g + 1):
+                    rows = pl.ds(8 * x, 8)
+                    found = [terms[x, 14 + i] for i in range(8)]
+                    total = tile(f, x) * (found[6] + diff[f] * found[7])
                     total = total + weighted(found[:6], diff[f], *[y_at(f, x, k) for k in (-2, -1, 1, 2)])
-                    if inner:
-                        total = total + weighted(found[12:18], diff[f], *[x_at(f, x, k) for k in (-2, -1, 1, 2)])
-                    total = total + weighted(found[6:12], diff[f], *z_all(f, x, here))
-                    out[f, pl.ds(8 * x, 8), :] = total
+                    out[f, rows, :] = out[f, rows, :] + total
             return carry
 
-        lax.fori_loop(0, fields // 2, one_field, 0)
+        lax.fori_loop(0, fields // 2, two_fields, 0)
 
     def edge_flux(first_x):
         kept = []
@@ -223,18 +246,18 @@
             qx[f, pl.ds(start + 8, 8), :] = cover
 
     return dict(
-        pick=pick, pack=pack, pad=pad, place=place, spread_halos=spread_halos, cell_weights=cell_weights,
-        main_flux=main_flux, ghost=ghost, use_ghost=use_ghost, edge_flux=edge_flux,
+        pick=pick, pack=pack, pad=pad, place=place, spread_z=spread_z, spread_y=spread_y, weights_zx=weights_zx,
+        weights_y=weights_y, flux_zx=flux_zx, flux_y=flux_y, ghost=ghost, use_ghost=use_ghost, edge_flux=edge_flux,
     )
 
 
 def kernel(
     n_x, n_y, n_z, fields,
-    fine, diff, coarse, sources, targets,
+    fine, diffusivity, coarse, sources, targets,
     out,
     qx, y_own, y_low, y_high, y_pad, z_own, z_low, z_high, z_rows,
     cells, src, tgt, msg, relay, arrived, order, spread, plane, terms,
-    load_sem, halo_send, halo_recv, row_send, row_recv, block_send, block_recv, pass_send, pass_recv, ready, open_sem,
+    diff, load_sem, halo_send, halo_recv, row_send, row_recv, block_send, block_recv, pass_send, pass_recv, ready, open_sem,
 ):
     a, b, c = lax.axis_index("gx"), lax.axis_index("gy"), lax.axis_index("gz")
     is_end = jnp.logical_or(a == 0, a == n_x - 1)
@@ -246,7 +269,7 @@
         cells, src, tgt, msg, relay, arrived, order, spread, plane, terms,
     )
 
-    n_early = n_y // 2
+    n_early = early_of(n_y)
     ends = (0, n_x - 1)
     corner = jnp.logical_and(jnp.logical_and(a == 0, b == 0), c == 0)
     is_first = jnp.logical_and(jnp.logical_and(is_end, b < n_early), jnp.logical_not(corner))
@@ -254,6 +277,8 @@
     is_late = jnp.logical_and(is_end, jnp.logical_not(is_first))
     with_corner = c == 0
     n_late = n_y - n_early
+    first_hub = n_early - n_hubs
+    hub_y = first_hub + lax.rem(b + (n_y * n_hubs - first_hub), n_hubs)
     row = lax.rem(b, n_hubs) * served + a * per_hub + lax.div(b, n_hubs)
 
     def x_at(k):
@@ -273,6 +298,8 @@
     load_src.start()
     load_fine.start()
     load_tgt.start()
+    load_diff = pltpu.make_async_copy(diffusivity, diff, load_sem.at[4])
+    load_diff.start()
 
     barrier = pltpu.get_barrier_semaphore()
 
@@ -330,7 +357,7 @@
         return pltpu.make_async_remote_copy(
             src_ref=msg.at[which, pl.ds(0, n_late + 1)], dst_ref=relay.at[slot],
             send_sem=block_send.at[which], recv_sem=block_recv,
-            device_id=(ends[which], n_early - n_hubs + lax.rem(b, n_hubs), c), device_id_type=MESH,
+            device_id=(ends[which], hub_y, c), device_id_type=MESH,
         )
 
     for peer in range(n_early):
@@ -350,7 +377,7 @@
                 arrived[pl.ds(row, 1)] = msg[which, pl.ds(n_late + peer, 1)]
 
     def own_hub(which):
-        return jnp.logical_and(a == ends[which], b == n_early - n_hubs + lax.rem(b, n_hubs))
+        return jnp.logical_and(a == ends[which], b == hub_y)
 
     for which in range(2):
 
@@ -365,7 +392,7 @@
     @pl.when(is_late)
     def _():
         for h in range(n_hubs):
-            pl.semaphore_signal(ready, inc=1, device_id=(a, n_early - n_hubs + h, c), device_id_type=MESH)
+            pl.semaphore_signal(ready, inc=1, device_id=(a, first_hub + h, c), device_id_type=MESH)
 
     def halo(i, source, target, device):
         return pltpu.make_async_remote_copy(
@@ -398,17 +425,18 @@
             pl.when(later)(functools.partial(send_later, i))
     halos = halos[:4]
     load_tgt.wait()
+    load_diff.wait()
 
     @pl.when(is_end)
     def _():
         step["place"]()
 
     step["pad"]()
-    for copy in halos:
+    for copy in halos[2:]:
         copy.wait_recv()
-    step["spread_halos"]()
-    step["cell_weights"]()
-    step["main_flux"]()
+    step["spread_z"]()
+    step["weights_zx"]()
+    step["flux_zx"]()
 
     @pl.when(has_high)
     def _():
@@ -419,11 +447,17 @@
     def _():
         to_high.wait_recv()
         step["edge_flux"](0)
+
+    for copy in halos[:2]:
+        copy.wait_recv()
+    step["spread_y"]()
+    step["weights_y"]()
+    step["flux_y"]()
 
     def to_late(peer):
         return pltpu.make_async_remote_copy(
             src_ref=relay.at[:, (peer - n_early) % n_y],
-            dst_ref=arrived.at[pl.ds((b - (n_early - n_hubs)) * served, served)],
+            dst_ref=arrived.at[pl.ds(lax.rem(b, n_hubs) * served, served)],
             send_sem=pass_send, recv_sem=pass_recv,
             device_id=(a, peer, c), device_id_type=MESH,
         )
@@ -471,8 +505,8 @@
 
     @pl.when(is_hub)
     def _():
-        for _ in range(n_late * served // peers):
-            rows_of(peers, pass_send, pass_recv).wait_send()
+        for _ in range(n_late):
+            rows_of(served, pass_send, pass_recv).wait_send()
 
         @pl.when(has_corner)
         def _():
@@ -522,7 +556,7 @@
         result = pl.pallas_call(
             functools.partial(kernel, n_x, n_y, n_z, fields),
             out_shape=pltpu.VMEM((fields, rows, cells_z), f32),
-            in_specs=[anywhere, pl.BlockSpec(memory_space=pltpu.SMEM), anywhere, anywhere, anywhere],
+            in_specs=[anywhere] * 5,
             out_specs=pl.BlockSpec(memory_space=pltpu.VMEM),
             scratch_shapes=[
                 vmem((fields, rows + 32, cells_z), f32),
@@ -538,13 +572,14 @@
                 vmem((3, 1, peers), jnp.int32),
                 vmem((3, 1, peers), jnp.int32),
                 vmem((2, n_y, 1, 128), f32),
-                vmem((n_x * per_hub, n_y - n_y // 2 + 1, 1, 128), f32),
+                vmem((n_x * per_hub, n_y - early_of(n_y) + 1, 1, 128), f32),
                 vmem((128, 1, 128), f32),
                 vmem((128, 128), f32),
                 vmem((384, 512), jnp.bfloat16),
                 vmem((8 * SLOT, 128), f32),
-                vmem((8, 20, 8, 128), f32),
-                pltpu.SemaphoreType.DMA((4,)),
+                vmem((8, 22, 8, 128), f32),
+                pltpu.SMEM((fields,), f32),
+                pltpu.SemaphoreType.DMA((5,)),
                 pltpu.SemaphoreType.DMA((6,)),
                 pltpu.SemaphoreType.DMA((6,)),
                 pltpu.SemaphoreType.DMA,

time: 24.1 us -> 21.9 us (0.909)
  Pallas kernels: 23.2 us -> 21 us
    pallas_call x1, Pallas kernels: 23.2 us -> 21 us  [on_device(): pl.pallas_call(functools.partial(kernel, n_x, n_y, n_z, fields), out_shap...]
where the time goes in v4:
time: 21.9 us; the launch traced here: 21.8 us
  Pallas kernels  21 us (96%)
  local copies, waits for them, and re-layouts  0.77 us (4%)
    pallas_call x1, Pallas kernels, on_device(): pl.pallas_call(functools.partial(kernel, n_x, n_y, n_z, fields), out_shap...  21 us
    unnamed x1, local copies, waits for them, and re-layouts  0.77 us

profile of v4, /device:TPU:1, one launch (start us, length us, event | category | flops | bytes accessed | tf_op | source)
XLA Modules:
  0.0 21.8 jit_solution(17540287071175178779)
XLA Ops:
  0.0 21.0 %shard_map.55 = f32[14,64,128]{2,1,0:T(8,128)S(1)} custom-call(f32[14,64,128]{2,1,0:T(8,128)} %bitcast.9, f32[14]{0:T(128)} %diffusivity.1, f32[14,128]{1,0:T(8,128)} %coarse.1, s32[3,1,96]{2,1,0:T(1,128)} %bitcast.10, s32[3,1,96]{2,1,0:T(1,128)} %bitcast.11), custom_call_target="tpu_custom_call" | custom-call | tf_op jit(solution)/shard_map/pallas_call | solution.py:556
  21.0 0.8 %copy.7 = f32[14,8,8,128]{3,2,1,0:T(8,128)} copy(f32[14,8,8,128]{3,2,1,0:T(8,128)S(1)} %bitcast.8) | data formatting | bytes 917504

commit v5 on v4

--- a/solution.py
+++ b/solution.py
@@ -13,12 +13,12 @@
 
 
 def hubs_of(n_y):
-    n_hubs = max(1, n_y // 4)
+    n_hubs = max(1, n_y // 6)
     return n_hubs, n_y // n_hubs
 
 
 def early_of(n_y):
-    return max(2, 5 * n_y // 12)
+    return max(2, n_y // 3)
 
 
 def split3(value):
@@ -69,14 +69,14 @@
 
 
 def work(n_x, n_y, fields, diff, out, qx, y_own, y_low, y_high, y_pad, z_own, z_low, z_high, z_rows,
-         cells, src, tgt, msg, relay, arrived, order, spread, plane, terms):
+         cells, src, tgt, msg, relay, merged, arrived, order, spread, plane, terms):
     peers = n_x * n_y
     n_hubs, per_hub = hubs_of(n_y)
     lane = lax.broadcasted_iota(jnp.int32, (8, 128), 1)
     line = lax.broadcasted_iota(jnp.int32, (8, 128), 0)
     blank = jnp.full((1, 128 - peers), -1, jnp.int32)
 
-    def pick():
+    def pick(upper):
         owned = jnp.concatenate([cells[...], jnp.zeros((SLOT - fields, 128), jnp.float32)], axis=0)
         owned = split3(owned)
         row = lax.broadcasted_iota(jnp.int32, (128, 128), 0)
@@ -86,8 +86,10 @@
             chosen = jnp.where(row == wanted, 1.0, 0.0).astype(jnp.bfloat16)
             part = jnp.dot(owned, chosen, preferred_element_type=jnp.float32)
             picked.append(part[:SLOT] + part[SLOT : 2 * SLOT] + part[2 * SLOT :])
-        picked.append(jnp.zeros((128 - 3 * SLOT, 128), jnp.float32))
-        picked = jnp.concatenate(picked, axis=0).T
+        none = jnp.zeros((SLOT, 128), jnp.float32)
+        low = jnp.concatenate(picked + [none] * 5, axis=0)
+        high = jnp.concatenate([none] * 4 + picked + [none], axis=0)
+        picked = jnp.where(upper, high, low).T
         n_early = early_of(n_y)
         for which, start in enumerate((0, peers - n_y)):
             msg[which, : n_y - n_early] = picked[start + n_early : start + n_y].reshape(n_y - n_early, 1, 128)
@@ -115,11 +117,12 @@
         wide.append(jnp.full((125, 128), -1, jnp.int32))
         wide = jnp.concatenate(wide, axis=0).astype(jnp.float32).T
         order[...] = jnp.full(order.shape, -1.0, jnp.float32)
-        count = n_x * per_hub
+        count = n_x // 2 * per_hub
         for a in range(n_x):
             for k in range(per_hub):
                 start = a * n_y + k * n_hubs
-                order[pl.ds(a * per_hub + k, n_hubs, stride=count), :] = wide[start : start + n_hubs]
+                first = 64 * (2 * a // n_x) + a % (n_x // 2) * per_hub + k
+                order[pl.ds(first, n_hubs, stride=count), :] = wide[start : start + n_hubs]
         half = (lax.broadcasted_iota(jnp.int32, (128, 128), 1) // 2).astype(jnp.float32)
         filled = order[...]
         for s in range(3):
@@ -129,7 +132,17 @@
                     cell - 64.0 * h == half, 1.0, 0.0
                 ).astype(jnp.bfloat16)
         if peers < 128:
-            arrived[peers:] = jnp.zeros((128 - peers, 1, 128), jnp.float32)
+            unused = jnp.zeros((64 - peers // 2, 1, 128), jnp.float32)
+            arrived[peers // 2 : 64] = unused
+            arrived[64 + peers // 2 :] = unused
+
+    def clear_upper():
+        arrived[64 : 64 + peers // 2] = jnp.zeros((peers // 2, 1, 128), jnp.float32)
+
+    def merge():
+        half = n_x // 2 * per_hub
+        for k in range(half):
+            merged[:, k] = relay[k] + relay[half + k]
 
     def tile(f, x):
         return qx[f, pl.ds(16 + 8 * x, 8), :]
@@ -231,8 +244,10 @@
                 out[f, rows, :] = out[f, rows, :] + total
 
     def ghost():
-        by_slot = arrived[...].reshape(128, 128).T
-        by_slot = jnp.concatenate([by_slot[SLOT * s : SLOT * (s + 1)] for s in range(3)], axis=1)
+        both = (arrived[:64] + arrived[64:]).reshape(64, 128)
+        both = jnp.concatenate([both, jnp.zeros((64, 128), jnp.float32)], axis=0).T
+        parts = [both[SLOT * i : SLOT * (i + 1), :64] for s in range(3) for i in (s, 4 + s)]
+        by_slot = jnp.concatenate(parts, axis=1)
         face = jnp.dot(split3(by_slot), spread[...], preferred_element_type=jnp.float32)
         face = face[:SLOT] + face[SLOT : 2 * SLOT] + face[2 * SLOT :]
         for y in range(8):
@@ -246,8 +261,9 @@
             qx[f, pl.ds(start + 8, 8), :] = cover
 
     return dict(
-        pick=pick, pack=pack, pad=pad, place=place, spread_z=spread_z, spread_y=spread_y, weights_zx=weights_zx,
-        weights_y=weights_y, flux_zx=flux_zx, flux_y=flux_y, ghost=ghost, use_ghost=use_ghost, edge_flux=edge_flux,
+        pick=pick, pack=pack, pad=pad, place=place, clear_upper=clear_upper, merge=merge, spread_z=spread_z,
+        spread_y=spread_y, weights_zx=weights_zx, weights_y=weights_y, flux_zx=flux_zx, flux_y=flux_y, ghost=ghost,
+        use_ghost=use_ghost, edge_flux=edge_flux,
     )
 
 
@@ -256,7 +272,7 @@
     fine, diffusivity, coarse, sources, targets,
     out,
     qx, y_own, y_low, y_high, y_pad, z_own, z_low, z_high, z_rows,
-    cells, src, tgt, msg, relay, arrived, order, spread, plane, terms,
+    cells, src, tgt, msg, relay, merged, arrived, order, spread, plane, terms,
     diff, load_sem, halo_send, halo_recv, row_send, row_recv, block_send, block_recv, pass_send, pass_recv, ready, open_sem,
 ):
     a, b, c = lax.axis_index("gx"), lax.axis_index("gy"), lax.axis_index("gz")
@@ -266,7 +282,7 @@
     served = n_x * per_hub
     step = work(
         n_x, n_y, fields, diff, out, qx, y_own, y_low, y_high, y_pad, z_own, z_low, z_high, z_rows,
-        cells, src, tgt, msg, relay, arrived, order, spread, plane, terms,
+        cells, src, tgt, msg, relay, merged, arrived, order, spread, plane, terms,
     )
 
     n_early = early_of(n_y)
@@ -279,7 +295,8 @@
     n_late = n_y - n_early
     first_hub = n_early - n_hubs
     hub_y = first_hub + lax.rem(b + (n_y * n_hubs - first_hub), n_hubs)
-    row = lax.rem(b, n_hubs) * served + a * per_hub + lax.div(b, n_hubs)
+    half_served = served // 2
+    row = 64 * lax.div(2 * a, n_x) + lax.rem(b, n_hubs) * half_served + lax.rem(a, n_x // 2) * per_hub + lax.div(b, n_hubs)
 
     def x_at(k):
         return (lax.rem(a + (k + n_x), n_x), b, c)
@@ -309,20 +326,24 @@
     has_low, has_high = a > 0, a < n_x - 1
     y_later = (b < n_y - 1, b == 0)
     z_later = (c < n_z // 2, jnp.logical_or(c == 0, c > n_z // 2))
+    mutual = b < n_y // 2
+    mutual_up, mutual_down = b < n_y // 2 - 1, jnp.logical_and(mutual, b > 0)
+
+    def either(p, q):
+        return jnp.logical_or(p, q)
+
     neighbours = [
-        (y_at(1), y_later[0], jnp.logical_not(y_later[0]), 1),
-        (y_at(-1), y_later[1], jnp.logical_not(y_later[1]), 0),
-        (z_at(1), z_later[0], jnp.logical_not(z_later[0]), 3),
-        (z_at(-1), z_later[1], jnp.logical_not(z_later[1]), 2),
-        (x_at(1), has_high, False, 5),
-        (x_at(-1), False, has_low, 4),
+        (y_at(1), either(jnp.logical_not(y_later[0]), mutual_up), either(y_later[0], mutual_up), 1),
+        (y_at(-1), either(jnp.logical_not(y_later[1]), mutual_down), either(y_later[1], mutual_down), 0),
+        (z_at(1), either(jnp.logical_not(z_later[0]), mutual), either(z_later[0], mutual), 3),
+        (z_at(-1), either(jnp.logical_not(z_later[1]), mutual), either(z_later[1], mutual), 2),
+        (x_at(1), jnp.logical_and(has_high, mutual), has_high, 5),
+        (x_at(-1), has_low, jnp.logical_and(has_low, mutual), 4),
     ]
-    n_earlier = 0
-    for device, later, earlier, _ in neighbours:
-        if later is not False:
-            pl.when(later)(functools.partial(greet, device))
-        if earlier is not False:
-            n_earlier = n_earlier + jnp.where(earlier, 1, 0)
+    n_greeting = 0
+    for device, greeting, greeted, _ in neighbours:
+        pl.when(greeted)(functools.partial(greet, device))
+        n_greeting = n_greeting + jnp.where(greeting, 1, 0)
 
     @pl.when(is_first)
     def _():
@@ -335,15 +356,14 @@
 
     load_cells.wait()
     load_src.wait()
-    step["pick"]()
-    pl.semaphore_wait(barrier, n_earlier + 2 * n_early - jnp.where(with_corner, 1, 0) - jnp.where(is_first, 1, 0))
+    step["pick"](a >= n_x // 2)
+    pl.semaphore_wait(barrier, n_greeting + 2 * n_early - jnp.where(with_corner, 1, 0) - jnp.where(is_first, 1, 0))
 
     def tell(device, number):
         pl.semaphore_signal(open_sem.at[number], inc=1, device_id=device, device_id_type=MESH)
 
-    for device, _, earlier, number in neighbours:
-        if earlier is not False:
-            pl.when(earlier)(functools.partial(tell, device, number))
+    for device, greeting, greeted, number in neighbours:
+        pl.when(jnp.logical_and(greeting, jnp.logical_not(greeted)))(functools.partial(tell, device, number))
 
     def to_first(which, peer):
         return pltpu.make_async_remote_copy(
@@ -416,13 +436,11 @@
         pl.semaphore_wait(open_sem.at[i], 1)
         halos[i].start()
 
-    for i, (_, _, earlier, _) in enumerate(neighbours):
-        if earlier is not False:
-            pl.when(earlier)(halos[i].start)
+    for i, (_, greeting, _, _) in enumerate(neighbours):
+        pl.when(greeting)(halos[i].start)
     for i in (5, 4, 3, 2, 0, 1):
-        later = neighbours[i][1]
-        if later is not False:
-            pl.when(later)(functools.partial(send_later, i))
+        unknown = jnp.logical_and(neighbours[i][2], jnp.logical_not(neighbours[i][1]))
+        pl.when(unknown)(functools.partial(send_later, i))
     halos = halos[:4]
     load_tgt.wait()
     load_diff.wait()
@@ -430,6 +448,11 @@
     @pl.when(is_end)
     def _():
         step["place"]()
+
+        @pl.when(is_late)
+        def _():
+            step["clear_upper"]()
+
 
     step["pad"]()
     for copy in halos[2:]:
@@ -456,8 +479,8 @@
 
     def to_late(peer):
         return pltpu.make_async_remote_copy(
-            src_ref=relay.at[:, (peer - n_early) % n_y],
-            dst_ref=arrived.at[pl.ds(lax.rem(b, n_hubs) * served, served)],
+            src_ref=merged.at[(peer - n_early) % n_y],
+            dst_ref=arrived.at[pl.ds(lax.rem(b, n_hubs) * half_served, half_served)],
             send_sem=pass_send, recv_sem=pass_recv,
             device_id=(a, peer, c), device_id_type=MESH,
         )
@@ -477,6 +500,7 @@
             src_ref=blocks, dst_ref=blocks, send_sem=block_send.at[0], recv_sem=block_recv,
             device_id=y_at(1), device_id_type=MESH,
         ).wait_recv()
+        step["merge"]()
         pl.semaphore_wait(ready, n_late + jnp.where(has_corner, 1, 0))
         for peer in range(n_early, n_y):
             to_late(peer).start()
@@ -491,7 +515,7 @@
 
     @pl.when(is_late)
     def _():
-        rows_of(peers, pass_send, pass_recv).wait_recv()
+        rows_of(peers // 2, pass_send, pass_recv).wait_recv()
 
     @pl.when(is_end)
     def _():
@@ -506,11 +530,11 @@
     @pl.when(is_hub)
     def _():
         for _ in range(n_late):
-            rows_of(served, pass_send, pass_recv).wait_send()
+            rows_of(half_served, pass_send, pass_recv).wait_send()
 
         @pl.when(has_corner)
         def _():
-            rows_of(served, pass_send, pass_recv).wait_send()
+            rows_of(half_served, pass_send, pass_recv).wait_send()
 
     rows_of(2 * n_early - 2, row_send, row_recv).wait_send()
 
@@ -573,6 +597,7 @@
                 vmem((3, 1, peers), jnp.int32),
                 vmem((2, n_y, 1, 128), f32),
                 vmem((n_x * per_hub, n_y - early_of(n_y) + 1, 1, 128), f32),
+                vmem((n_y - early_of(n_y) + 1, n_x // 2 * per_hub, 1, 128), f32),
                 vmem((128, 1, 128), f32),
                 vmem((128, 128), f32),
                 vmem((384, 512), jnp.bfloat16),

time: 21.9 us -> 22 us (level)
  no operation moved by 1% of the time
where the time goes in v5:
time: 22 us; the launch traced here: 21.9 us
  Pallas kernels  21.1 us (96%)
  local copies, waits for them, and re-layouts  0.77 us (4%)
    pallas_call x1, Pallas kernels, on_device(): pl.pallas_call(functools.partial(kernel, n_x, n_y, n_z, fields), out_shap...  21.1 us
    unnamed x1, local copies, waits for them, and re-layouts  0.77 us

profile of v5, /device:TPU:1, one launch (start us, length us, event | category | flops | bytes accessed | tf_op | source)
XLA Modules:
  0.0 21.9 jit_solution(849205720137500906)
XLA Ops:
  0.0 21.1 %shard_map.55 = f32[14,64,128]{2,1,0:T(8,128)S(1)} custom-call(f32[14,64,128]{2,1,0:T(8,128)} %bitcast.9, f32[14]{0:T(128)} %diffusivity.1, f32[14,128]{1,0:T(8,128)} %coarse.1, s32[3,1,96]{2,1,0:T(1,128)} %bitcast.10, s32[3,1,96]{2,1,0:T(1,128)} %bitcast.11), custom_call_target="tpu_custom_call" | custom-call | tf_op jit(solution)/shard_map/pallas_call | solution.py:580
  21.1 0.8 %copy.7 = f32[14,8,8,128]{3,2,1,0:T(8,128)} copy(f32[14,8,8,128]{3,2,1,0:T(8,128)S(1)} %bitcast.8) | data formatting | bytes 917504

commit v6 on v5

--- a/solution.py
+++ b/solution.py
@@ -245,8 +245,8 @@
 
     def ghost():
         both = (arrived[:64] + arrived[64:]).reshape(64, 128)
-        both = jnp.concatenate([both, jnp.zeros((64, 128), jnp.float32)], axis=0).T
-        parts = [both[SLOT * i : SLOT * (i + 1), :64] for s in range(3) for i in (s, 4 + s)]
+        both = both.T
+        parts = [both[SLOT * i : SLOT * (i + 1)] for s in range(3) for i in (s, 4 + s)]
         by_slot = jnp.concatenate(parts, axis=1)
         face = jnp.dot(split3(by_slot), spread[...], preferred_element_type=jnp.float32)
         face = face[:SLOT] + face[SLOT : 2 * SLOT] + face[2 * SLOT :]
@@ -254,16 +254,25 @@
             h = y // 2
             plane[SLOT * y : SLOT * (y + 1), :] = face[:, 128 * h : 128 * (h + 1)]
 
-    def use_ghost(start):
+    def ghost_flux(first_x):
+        def at(f, x):
+            if 0 <= x < 8:
+                return tile(f, x)
+            return plane[pl.ds(f, 8, stride=SLOT), :]
+
+        planes = (first_x, first_x + 1)
+        weights = [three([at(9, x + k) for k in (-1, 0, 1)], [at(10, x + k) for k in (-1, 0, 1)]) for x in planes]
         for f in range(fields):
-            cover = plane[pl.ds(f, 8, stride=SLOT), :]
-            qx[f, pl.ds(start, 8), :] = cover
-            qx[f, pl.ds(start + 8, 8), :] = cover
+            for x, (found, (centre, d_centre)) in zip(planes, weights):
+                rows = pl.ds(8 * x, 8)
+                total = tile(f, x) * (centre + diff[f] * d_centre)
+                total = total + weighted(found, diff[f], *[at(f, x + k) for k in (-2, -1, 1, 2)])
+                out[f, rows, :] = out[f, rows, :] + total
 
     return dict(
         pick=pick, pack=pack, pad=pad, place=place, clear_upper=clear_upper, merge=merge, spread_z=spread_z,
         spread_y=spread_y, weights_zx=weights_zx, weights_y=weights_y, flux_zx=flux_zx, flux_y=flux_y, ghost=ghost,
-        use_ghost=use_ghost, edge_flux=edge_flux,
+        ghost_flux=ghost_flux, edge_flux=edge_flux,
     )
 
 
@@ -313,10 +322,6 @@
     load_tgt = pltpu.make_async_copy(targets, tgt, load_sem.at[3])
     load_cells.start()
     load_src.start()
-    load_fine.start()
-    load_tgt.start()
-    load_diff = pltpu.make_async_copy(diffusivity, diff, load_sem.at[4])
-    load_diff.start()
 
     barrier = pltpu.get_barrier_semaphore()
 
@@ -345,6 +350,11 @@
         pl.when(greeted)(functools.partial(greet, device))
         n_greeting = n_greeting + jnp.where(greeting, 1, 0)
 
+    load_fine.start()
+    load_tgt.start()
+    load_diff = pltpu.make_async_copy(diffusivity, diff, load_sem.at[4])
+    load_diff.start()
+
     @pl.when(is_first)
     def _():
         for k in range(n_x):
@@ -380,8 +390,8 @@
             device_id=(ends[which], hub_y, c), device_id_type=MESH,
         )
 
-    for peer in range(n_early):
-        for which in range(2):
+    for which in range(2):
+        for peer in sorted(range(n_early), key=lambda p: p ^ 1):
             itself = jnp.logical_and(a == ends[which], b == peer)
             meant = jnp.logical_not(itself)
             if peer == 0 and which == 0:
@@ -477,18 +487,45 @@
     step["weights_y"]()
     step["flux_y"]()
 
+    def rows_of(count, send, recv):
+        rows = arrived.at[pl.ds(0, count)]
+        return pltpu.make_async_remote_copy(
+            src_ref=rows, dst_ref=rows, send_sem=send, recv_sem=recv, device_id=y_at(1), device_id_type=MESH
+        )
+
+    rows_of(2 * n_early - 2, row_send, row_recv).wait_send()
+
+    @pl.when(jnp.logical_not(is_first))
+    def _():
+        rows_of(1, row_send, row_recv).wait_send()
+
+    @pl.when(jnp.logical_not(with_corner))
+    def _():
+        rows_of(1, row_send, row_recv).wait_send()
+
+    for which in range(2):
+
+        @pl.when(jnp.logical_not(own_hub(which)))
+        def _():
+            to_hub(which).wait_send()
+
+    for copy in halos:
+        copy.wait_send()
+
+    @pl.when(has_low)
+    def _():
+        to_low.wait_send()
+
+    @pl.when(has_high)
+    def _():
+        to_high.wait_send()
+
     def to_late(peer):
         return pltpu.make_async_remote_copy(
             src_ref=merged.at[(peer - n_early) % n_y],
             dst_ref=arrived.at[pl.ds(lax.rem(b, n_hubs) * half_served, half_served)],
             send_sem=pass_send, recv_sem=pass_recv,
             device_id=(a, peer, c), device_id_type=MESH,
-        )
-
-    def rows_of(count, send, recv):
-        rows = arrived.at[pl.ds(0, count)]
-        return pltpu.make_async_remote_copy(
-            src_ref=rows, dst_ref=rows, send_sem=send, recv_sem=recv, device_id=y_at(1), device_id_type=MESH
         )
 
     has_corner = jnp.logical_and(with_corner, a == 0)
@@ -520,12 +557,8 @@
     @pl.when(is_end)
     def _():
         step["ghost"]()
-        for end, start, first_x in ((0, 0, 0), (n_x - 1, 80, 6)):
-
-            @pl.when(a == end)
-            def _():
-                step["use_ghost"](start)
-                step["edge_flux"](first_x)
+        pl.when(a == 0)(functools.partial(step["ghost_flux"], 0))
+        pl.when(a == n_x - 1)(functools.partial(step["ghost_flux"], 6))
 
     @pl.when(is_hub)
     def _():
@@ -535,33 +568,6 @@
         @pl.when(has_corner)
         def _():
             rows_of(half_served, pass_send, pass_recv).wait_send()
-
-    rows_of(2 * n_early - 2, row_send, row_recv).wait_send()
-
-    @pl.when(jnp.logical_not(is_first))
-    def _():
-        rows_of(1, row_send, row_recv).wait_send()
-
-    @pl.when(jnp.logical_not(with_corner))
-    def _():
-        rows_of(1, row_send, row_recv).wait_send()
-
-    for which in range(2):
-
-        @pl.when(jnp.logical_not(own_hub(which)))
-        def _():
-            to_hub(which).wait_send()
-
-    for copy in halos:
-        copy.wait_send()
-
-    @pl.when(has_low)
-    def _():
-        to_low.wait_send()
-
-    @pl.when(has_high)
-    def _():
-        to_high.wait_send()
 
 
 def solution(mesh):

time: 22 us -> 22 us (level)
  no operation moved by 1% of the time
where the time goes in v6:
time: 22 us; the launch traced here: 21.8 us
  Pallas kernels  21.1 us (96%)
  local copies, waits for them, and re-layouts  0.77 us (4%)
    pallas_call x1, Pallas kernels, on_device(): pl.pallas_call(functools.partial(kernel, n_x, n_y, n_z, fields), out_shap...  21.1 us
    unnamed x1, local copies, waits for them, and re-layouts  0.77 us

profile of v6, /device:TPU:1, one launch (start us, length us, event | category | flops | bytes accessed | tf_op | source)
XLA Modules:
  0.0 21.8 jit_solution(2537006522504172209)
XLA Ops:
  0.0 21.1 %shard_map.55 = f32[14,64,128]{2,1,0:T(8,128)S(1)} custom-call(f32[14,64,128]{2,1,0:T(8,128)} %bitcast.9, f32[14]{0:T(128)} %diffusivity.1, f32[14,128]{1,0:T(8,128)} %coarse.1, s32[3,1,96]{2,1,0:T(1,128)} %bitcast.10, s32[3,1,96]{2,1,0:T(1,128)} %bitcast.11), custom_call_target="tpu_custom_call" | custom-call | tf_op jit(solution)/shard_map/pallas_call | solution.py:586
  21.1 0.8 %copy.7 = f32[14,8,8,128]{3,2,1,0:T(8,128)} copy(f32[14,8,8,128]{3,2,1,0:T(8,128)S(1)} %bitcast.8) | data formatting | bytes 917504

commit v7 on v6

--- a/solution.py
+++ b/solution.py
@@ -357,8 +357,8 @@
 
     @pl.when(is_first)
     def _():
-        for k in range(n_x):
-            for peer in range(n_y):
+        for peer in sorted(range(n_y), key=lambda p: (p + n_y // 2) % n_y):
+            for k in range(n_x):
 
                 @pl.when(jnp.logical_or(a != k, b != peer))
                 def _():

time: 22 us -> 22 us (level)
  no operation moved by 1% of the time
where the time goes in v7:
time: 22 us; the launch traced here: 21.8 us
  Pallas kernels  21.1 us (96%)
  local copies, waits for them, and re-layouts  0.77 us (4%)
    pallas_call x1, Pallas kernels, on_device(): pl.pallas_call(functools.partial(kernel, n_x, n_y, n_z, fields), out_shap...  21.1 us
    unnamed x1, local copies, waits for them, and re-layouts  0.77 us

profile of v7, /device:TPU:1, one launch (start us, length us, event | category | flops | bytes accessed | tf_op | source)
XLA Modules:
  0.0 21.8 jit_solution(9645470169175244539)
XLA Ops:
  0.0 21.1 %shard_map.55 = f32[14,64,128]{2,1,0:T(8,128)S(1)} custom-call(f32[14,64,128]{2,1,0:T(8,128)} %bitcast.9, f32[14]{0:T(128)} %diffusivity.1, f32[14,128]{1,0:T(8,128)} %coarse.1, s32[3,1,96]{2,1,0:T(1,128)} %bitcast.10, s32[3,1,96]{2,1,0:T(1,128)} %bitcast.11), custom_call_target="tpu_custom_call" | custom-call | tf_op jit(solution)/shard_map/pallas_call | solution.py:586
  21.1 0.8 %copy.7 = f32[14,8,8,128]{3,2,1,0:T(8,128)} copy(f32[14,8,8,128]{3,2,1,0:T(8,128)S(1)} %bitcast.8) | data formatting | bytes 917504

commit v8 on v6

--- a/solution.py
+++ b/solution.py
@@ -350,7 +350,6 @@
         pl.when(greeted)(functools.partial(greet, device))
         n_greeting = n_greeting + jnp.where(greeting, 1, 0)
 
-    load_fine.start()
     load_tgt.start()
     load_diff = pltpu.make_async_copy(diffusivity, diff, load_sem.at[4])
     load_diff.start()
@@ -366,6 +365,7 @@
 
     load_cells.wait()
     load_src.wait()
+    load_fine.start()
     step["pick"](a >= n_x // 2)
     pl.semaphore_wait(barrier, n_greeting + 2 * n_early - jnp.where(with_corner, 1, 0) - jnp.where(is_first, 1, 0))
 

time: 22 us -> 22 us (level)
  no operation moved by 1% of the time
where the time goes in v8:
time: 22 us; the launch traced here: 21.8 us
  Pallas kernels  21.1 us (96%)
  local copies, waits for them, and re-layouts  0.77 us (4%)
    pallas_call x1, Pallas kernels, on_device(): pl.pallas_call(functools.partial(kernel, n_x, n_y, n_z, fields), out_shap...  21.1 us
    unnamed x1, local copies, waits for them, and re-layouts  0.77 us

profile of v8, /device:TPU:1, one launch (start us, length us, event | category | flops | bytes accessed | tf_op | source)
XLA Modules:
  0.0 21.8 jit_solution(17659625396415123610)
XLA Ops:
  0.0 21.1 %shard_map.55 = f32[14,64,128]{2,1,0:T(8,128)S(1)} custom-call(f32[14,64,128]{2,1,0:T(8,128)} %bitcast.9, f32[14]{0:T(128)} %diffusivity.1, f32[14,128]{1,0:T(8,128)} %coarse.1, s32[3,1,96]{2,1,0:T(1,128)} %bitcast.10, s32[3,1,96]{2,1,0:T(1,128)} %bitcast.11), custom_call_target="tpu_custom_call" | custom-call | tf_op jit(solution)/shard_map/pallas_call | solution.py:586
  21.1 0.8 %copy.7 = f32[14,8,8,128]{3,2,1,0:T(8,128)} copy(f32[14,8,8,128]{3,2,1,0:T(8,128)S(1)} %bitcast.8) | data formatting | bytes 917504
